TPU v7x, 128 devices: a whole 4x4x4 slice. The times are simulated.
128 devices in a mesh: alpha: 16 (over x, z), beta: 8 (over y, core).
Axes of the slice: x: 4, y: 4, z: 4, core: 2. Of those that a mesh axis runs over, the one named last changes fastest.
Arguments:
- amplitudes: bfloat16 [8192, 256], P('alpha', 'beta'), may hold values from -6 to 6
- integrals: float32 [324, 324], replicated, may hold values from -0.1 to 0.1
- beta_pair: int32 [256, 256], P('beta'), may hold values from 0 to 323
- beta_coef: float32 [256, 256], P('beta'), may hold values from -1 to 1, as said below
- pair_src: int32 [64, 4], replicated, may hold values from 0 to 63, as said below
- link_row: int32 [64, 4, 1024], P('alpha'), may hold values from 0 to 127
- link_col: int32 [64, 4, 1024], P('alpha'), may hold values from 0 to 41471
- link_coef: float32 [64, 4, 1024], P('alpha'), may hold values from -1 to 1, as said below
- link_count: int32 [64, 4], P('alpha'), may hold values from 512 to 1024, as said below
Outputs:
- sigma: float32 [8192, 256], P('alpha', 'beta')
Inputs may be any that keep to these rules, and one draw needn't show every extreme that they name: `beta_coef`: each entry is -1, 0 or 1. `link_coef`: each entry is -1 or 1. `pair_src`: block b is held by alpha device b // 4. Each row names 4 different blocks. The rows of the 4 target blocks of one alpha device together name at most 2 different blocks held by any one alpha device, and exactly 2 for some holder in every draw. `link_count`: some block pair has all 1024 slots occupied in every draw.
All inputs are finite; a program needn't handle non-finite values.
Results may differ from a plain program's by a relative error of at most 0.0029.
Values may be sent and summed in bfloat16 or wider, within the bound.
A program may use at most 128 MiB of HBM per device.

v0:
```python
import jax
import jax.numpy as jnp
from jax import lax
from jax.sharding import PartitionSpec as P

NP = 324
ABLK = 128
LINKS = 1024
FETCH_CAP = 2


def assemble(local_amp, pair_src, num_local):
    alpha_count = lax.axis_size("alpha")
    my_index = lax.axis_index("alpha")
    block_total = pair_src.shape[0]
    block_rows = local_amp.shape[1]
    slab_width = local_amp.shape[2]
    my_requests = lax.dynamic_slice_in_dim(pair_src, my_index * num_local, num_local, 0)
    owned_ids = my_index * num_local + jnp.arange(num_local, dtype=jnp.int32)
    requests = pair_src.reshape(alpha_count, -1)
    asked_for = jnp.any(requests[:, :, None] == owned_ids[None, None, :], axis=1)
    position = jnp.cumsum(asked_for.astype(jnp.int32), axis=1) - 1
    slot_ids = jnp.arange(FETCH_CAP, dtype=jnp.int32)
    select = (asked_for[:, None, :] & (position[:, None, :] == slot_ids[None, :, None])).astype(
        local_amp.dtype
    )
    outgoing = jnp.einsum(
        "qsj,jab->qsab", select, local_amp, preferred_element_type=jnp.float32
    ).astype(local_amp.dtype)
    incoming = lax.all_to_all(outgoing, "alpha", split_axis=0, concat_axis=0, tiled=True)
    combined = jnp.concatenate([local_amp, incoming.reshape(-1, block_rows, slab_width)], axis=0)
    catalog = jnp.arange(block_total, dtype=jnp.int32).reshape(alpha_count, num_local)
    wanted = jnp.any(my_requests.reshape(-1)[:, None, None] == catalog[None], axis=0)
    order_pos = jnp.cumsum(wanted.astype(jnp.int32), axis=1) - 1
    owner_dev = my_requests // num_local
    within = my_requests % num_local
    remote = num_local + owner_dev * FETCH_CAP + order_pos[owner_dev, within]
    return (combined, jnp.where(owner_dev == my_index, within, remote))


def body(
    amplitudes, integrals, beta_pair, beta_coef, pair_src, link_row, link_col, link_coef, link_count
):
    num_local = link_row.shape[0]
    slab_piece = amplitudes.shape[1]
    local_amp = amplitudes.reshape(num_local, ABLK, slab_piece)
    full_rows = lax.all_gather(local_amp, "beta", axis=2, tiled=True)
    gathered, sources = assemble(full_rows, pair_src, num_local)
    pair_ids = jnp.arange(NP, dtype=jnp.int32)
    pair_hot = (beta_pair[None, :, :] == pair_ids[:, None, None]).astype(jnp.float32)
    looked_up = jnp.einsum("ki,ibj->kbj", integrals, pair_hot, precision=lax.Precision.HIGHEST)
    coupled = (looked_up * beta_coef[None]).astype(jnp.bfloat16)
    link_ids = jnp.arange(LINKS, dtype=jnp.int32)
    string_ids = jnp.arange(ABLK, dtype=jnp.int32)

    def per_target(target, sigma_acc):
        chosen = lax.dynamic_index_in_dim(sources, target, 0, keepdims=False)
        columns = lax.dynamic_index_in_dim(link_col, target, 0, keepdims=False)
        occupied = lax.dynamic_index_in_dim(link_count, target, 0, keepdims=False)
        signs = lax.dynamic_index_in_dim(link_coef, target, 0, keepdims=False)
        targets_row = lax.dynamic_index_in_dim(link_row, target, 0, keepdims=False)

        def per_pair(total, pair_index):
            block = jnp.take(gathered, chosen[pair_index], axis=0)
            column_row = columns[pair_index]
            orbital_pair = column_row // ABLK
            source_row = column_row % ABLK
            amp_rows = jnp.take(block, source_row, axis=0)
            coupled_rows = jnp.take(coupled, orbital_pair, axis=0)
            picked = jnp.einsum(
                "lbj,lj->lb", coupled_rows, amp_rows, preferred_element_type=jnp.float32
            )
            weights = jnp.where(
                link_ids < occupied[pair_index], signs[pair_index], jnp.float32(0.0)
            )
            hot_rows = (targets_row[pair_index][:, None] == string_ids[None, :]).astype(jnp.float32)
            added = jnp.dot(
                hot_rows.T,
                picked * weights[:, None],
                precision=lax.Precision.HIGHEST,
                preferred_element_type=jnp.float32,
            )
            return (total + added, None)

        start = jnp.zeros((ABLK, slab_piece), jnp.float32)
        result, unused = lax.scan(per_pair, start, jnp.arange(chosen.shape[0], dtype=jnp.int32))
        return lax.dynamic_update_index_in_dim(sigma_acc, result, target, 0)

    sigma_acc = jnp.zeros((num_local, ABLK, slab_piece), jnp.float32)
    sigma_acc = lax.fori_loop(0, num_local, per_target, sigma_acc)
    return sigma_acc.reshape(num_local * ABLK, slab_piece)


def solution(mesh):
    in_specs = (
        P("alpha", "beta"),
        P(),
        P("beta", None),
        P("beta", None),
        P(),
        P("alpha", None, None),
        P("alpha", None, None),
        P("alpha", None, None),
        P("alpha", None),
    )
    out_specs = P("alpha", "beta")
    return jax.shard_map(body, mesh=mesh, in_specs=in_specs, out_specs=out_specs, check_vma=False)
```

profile of v0, /device:TPU:1, one launch (start us, length us, event | category | flops | bytes accessed | tf_op | source)
XLA Modules:
  0.0 668.8 jit_solution(4186078040593497263)
XLA Ops:
  2.0 14.7 %all_gather.3 = bf16[4,128,256]{1,0,2:T(4,128)(2,1)S(1)} all-gather(bf16[4,128,32]{1,0,2:T(4,128)(2,1)S(1)} %reshape.206), channel_id=1, replica_groups=mesh['alpha'=16,'beta'=8] {'beta'}, dimensions={2}, use_global_device_ids=true | all-gather | bytes 294912 | tf_op jit(solution)/shard_map/all_gather | solution.py:47
  42.4 14.1 %all-to-all-done = bf16[16,2,128,256]{3,2,1,0:T(8,128)(2,1)S(1)} async-done(((bf16[16,2,128,256]{3,2,1,0:T(8,128)(2,1)}), bf16[16,2,128,256]{3,2,1,0:T(8,128)(2,1)S(1)}, u32[]{:S(2)}, u32[]{:S(2)}) %all-to-all-start) | async-done | bytes 2097184 | tf_op jit(solution)/shard_map/all_to_all | solution.py:30
  58.2 609.1 %while.51 = (s32[]{:T(128)}, f32[4,128,32]{1,0,2:T(4,128)}, s32[4,4]{1,0:T(4,128)}, s32[4,4,1024]{2,1,0:T(4,128)}, s32[4,4]{1,0:T(4,128)}, /*index=5*/f32[4,4,10...) while((s32[]{:T(128)}, f32[4,128,32]{1,0,2:T(4,128)}, ...), condition=%wide.region_7.8_spmd.clone, body=%wide.region_4.7_spmd.clone.sunk | while | flops 76029968 | bytes 53614264 | solution.py:90
  60.4 148.6 %while.52 = (s32[]{:T(128)}, f32[128,32]{0,1:T(8,128)S(1)}, s32[4]{0:T(128)S(1)}, s32[4,1024]{1,0:T(4,128)S(1)}, s32[128]{0:T(128)S(1)}, /*index=5*/s32[4,1024]{...) while((s32[]{:T(128)}, f32[128,32]{0,1:T(8,128)S(1)}, ...), condition=%wide.region_6.6_spmd.clone, body=%wide.region_5.5_spmd.clone.sunk | while | flops 76029968 | bytes 53478196 | solution.py:86
  70.1 14.9 %gather_fusion = bf16[1024,32,256]{2,1,0:T(8,128)(2,1)} fusion(bf16[324,32,256]{2,1,0:T(8,128)(2,1)} %get-tuple-element.835, s32[1024]{0:T(1024)S(1)} %broadcast_clamp_fusion.4), kind=kCustom, calls=%fused_computation.clone.clone.1 | custom fusion | bytes 33558528 | tf_op jit(solution)/shard_map/while/body/eval_jaxpr/while/body/eval_jaxpr/jit(_take)/gather | solution.py:69
  85.0 10.5 %fusion.46 = f32[1024,1,32]{2,1,0:T(1,128)S(1)} fusion(bf16[1024,32,256]{2,1,0:T(8,128)(2,1)} %gather_fusion, pred[1024]{0:T(1024)(128)(4,1)S(1)} %get-tuple-element.792, bf16[1024,256,1]{1,0,2:T(8,128)(2,1)S(1)} %select_bitcast_fusion.5), kind=kOutput, calls=%fused_computation.5.clone.1 | convolution fusion | flops 25165824 | bytes 17433600 | tf_op jit(solution)/shard_map/while/body/eval_jaxpr/while/body/eval_jaxpr/lbj,lj->lb/dot_general | solution.py:70
  107.2 14.9 %gather_fusion = bf16[1024,32,256]{2,1,0:T(8,128)(2,1)} fusion(bf16[324,32,256]{2,1,0:T(8,128)(2,1)} %get-tuple-element.835, s32[1024]{0:T(1024)S(1)} %broadcast_clamp_fusion.4), kind=kCustom, calls=%fused_computation.clone.clone.1 | custom fusion | bytes 33558528 | tf_op jit(solution)/shard_map/while/body/eval_jaxpr/while/body/eval_jaxpr/jit(_take)/gather | solution.py:69
  144.3 14.9 %gather_fusion = bf16[1024,32,256]{2,1,0:T(8,128)(2,1)} fusion(bf16[324,32,256]{2,1,0:T(8,128)(2,1)} %get-tuple-element.835, s32[1024]{0:T(1024)S(1)} %broadcast_clamp_fusion.4), kind=kCustom, calls=%fused_computation.clone.clone.1 | custom fusion | bytes 33558528 | tf_op jit(solution)/shard_map/while/body/eval_jaxpr/while/body/eval_jaxpr/jit(_take)/gather | solution.py:69
  181.5 14.9 %gather_fusion = bf16[1024,32,256]{2,1,0:T(8,128)(2,1)} fusion(bf16[324,32,256]{2,1,0:T(8,128)(2,1)} %get-tuple-element.835, s32[1024]{0:T(1024)S(1)} %broadcast_clamp_fusion.4), kind=kCustom, calls=%fused_computation.clone.clone.1 | custom fusion | bytes 33558528 | tf_op jit(solution)/shard_map/while/body/eval_jaxpr/while/body/eval_jaxpr/jit(_take)/gather | solution.py:69
  212.7 148.6 %while.52 = (s32[]{:T(128)}, f32[128,32]{0,1:T(8,128)S(1)}, s32[4]{0:T(128)S(1)}, s32[4,1024]{1,0:T(4,128)S(1)}, s32[128]{0:T(128)S(1)}, /*index=5*/s32[4,1024]{...) while((s32[]{:T(128)}, f32[128,32]{0,1:T(8,128)S(1)}, ...), condition=%wide.region_6.6_spmd.clone, body=%wide.region_5.5_spmd.clone.sunk | while | flops 76029968 | bytes 53478196 | solution.py:86
  222.3 14.9 %gather_fusion = bf16[1024,32,256]{2,1,0:T(8,128)(2,1)} fusion(bf16[324,32,256]{2,1,0:T(8,128)(2,1)} %get-tuple-element.835, s32[1024]{0:T(1024)S(1)} %broadcast_clamp_fusion.4), kind=kCustom, calls=%fused_computation.clone.clone.1 | custom fusion | bytes 33558528 | tf_op jit(solution)/shard_map/while/body/eval_jaxpr/while/body/eval_jaxpr/jit(_take)/gather | solution.py:69
  259.5 14.9 %gather_fusion = bf16[1024,32,256]{2,1,0:T(8,128)(2,1)} fusion(bf16[324,32,256]{2,1,0:T(8,128)(2,1)} %get-tuple-element.835, s32[1024]{0:T(1024)S(1)} %broadcast_clamp_fusion.4), kind=kCustom, calls=%fused_computation.clone.clone.1 | custom fusion | bytes 33558528 | tf_op jit(solution)/shard_map/while/body/eval_jaxpr/while/body/eval_jaxpr/jit(_take)/gather | solution.py:69
  296.6 14.9 %gather_fusion = bf16[1024,32,256]{2,1,0:T(8,128)(2,1)} fusion(bf16[324,32,256]{2,1,0:T(8,128)(2,1)} %get-tuple-element.835, s32[1024]{0:T(1024)S(1)} %broadcast_clamp_fusion.4), kind=kCustom, calls=%fused_computation.clone.clone.1 | custom fusion | bytes 33558528 | tf_op jit(solution)/shard_map/while/body/eval_jaxpr/while/body/eval_jaxpr/jit(_take)/gather | solution.py:69
  333.7 14.9 %gather_fusion = bf16[1024,32,256]{2,1,0:T(8,128)(2,1)} fusion(bf16[324,32,256]{2,1,0:T(8,128)(2,1)} %get-tuple-element.835, s32[1024]{0:T(1024)S(1)} %broadcast_clamp_fusion.4), kind=kCustom, calls=%fused_computation.clone.clone.1 | custom fusion | bytes 33558528 | tf_op jit(solution)/shard_map/while/body/eval_jaxpr/while/body/eval_jaxpr/jit(_take)/gather | solution.py:69
  364.9 148.6 %while.52 = (s32[]{:T(128)}, f32[128,32]{0,1:T(8,128)S(1)}, s32[4]{0:T(128)S(1)}, s32[4,1024]{1,0:T(4,128)S(1)}, s32[128]{0:T(128)S(1)}, /*index=5*/s32[4,1024]{...) while((s32[]{:T(128)}, f32[128,32]{0,1:T(8,128)S(1)}, ...), condition=%wide.region_6.6_spmd.clone, body=%wide.region_5.5_spmd.clone.sunk | while | flops 76029968 | bytes 53478196 | solution.py:86
  374.6 14.9 %gather_fusion = bf16[1024,32,256]{2,1,0:T(8,128)(2,1)} fusion(bf16[324,32,256]{2,1,0:T(8,128)(2,1)} %get-tuple-element.835, s32[1024]{0:T(1024)S(1)} %broadcast_clamp_fusion.4), kind=kCustom, calls=%fused_computation.clone.clone.1 | custom fusion | bytes 33558528 | tf_op jit(solution)/shard_map/while/body/eval_jaxpr/while/body/eval_jaxpr/jit(_take)/gather | solution.py:69
  411.7 14.9 %gather_fusion = bf16[1024,32,256]{2,1,0:T(8,128)(2,1)} fusion(bf16[324,32,256]{2,1,0:T(8,128)(2,1)} %get-tuple-element.835, s32[1024]{0:T(1024)S(1)} %broadcast_clamp_fusion.4), kind=kCustom, calls=%fused_computation.clone.clone.1 | custom fusion | bytes 33558528 | tf_op jit(solution)/shard_map/while/body/eval_jaxpr/while/body/eval_jaxpr/jit(_take)/gather | solution.py:69
  448.9 14.9 %gather_fusion = bf16[1024,32,256]{2,1,0:T(8,128)(2,1)} fusion(bf16[324,32,256]{2,1,0:T(8,128)(2,1)} %get-tuple-element.835, s32[1024]{0:T(1024)S(1)} %broadcast_clamp_fusion.4), kind=kCustom, calls=%fused_computation.clone.clone.1 | custom fusion | bytes 33558528 | tf_op jit(solution)/shard_map/while/body/eval_jaxpr/while/body/eval_jaxpr/jit(_take)/gather | solution.py:69
  486.0 14.9 %gather_fusion = bf16[1024,32,256]{2,1,0:T(8,128)(2,1)} fusion(bf16[324,32,256]{2,1,0:T(8,128)(2,1)} %get-tuple-element.835, s32[1024]{0:T(1024)S(1)} %broadcast_clamp_fusion.4), kind=kCustom, calls=%fused_computation.clone.clone.1 | custom fusion | bytes 33558528 | tf_op jit(solution)/shard_map/while/body/eval_jaxpr/while/body/eval_jaxpr/jit(_take)/gather | solution.py:69
  517.2 148.6 %while.52 = (s32[]{:T(128)}, f32[128,32]{0,1:T(8,128)S(1)}, s32[4]{0:T(128)S(1)}, s32[4,1024]{1,0:T(4,128)S(1)}, s32[128]{0:T(128)S(1)}, /*index=5*/s32[4,1024]{...) while((s32[]{:T(128)}, f32[128,32]{0,1:T(8,128)S(1)}, ...), condition=%wide.region_6.6_spmd.clone, body=%wide.region_5.5_spmd.clone.sunk | while | flops 76029968 | bytes 53478196 | solution.py:86
  526.9 14.9 %gather_fusion = bf16[1024,32,256]{2,1,0:T(8,128)(2,1)} fusion(bf16[324,32,256]{2,1,0:T(8,128)(2,1)} %get-tuple-element.835, s32[1024]{0:T(1024)S(1)} %broadcast_clamp_fusion.4), kind=kCustom, calls=%fused_computation.clone.clone.1 | custom fusion | bytes 33558528 | tf_op jit(solution)/shard_map/while/body/eval_jaxpr/while/body/eval_jaxpr/jit(_take)/gather | solution.py:69
  564.0 14.9 %gather_fusion = bf16[1024,32,256]{2,1,0:T(8,128)(2,1)} fusion(bf16[324,32,256]{2,1,0:T(8,128)(2,1)} %get-tuple-element.835, s32[1024]{0:T(1024)S(1)} %broadcast_clamp_fusion.4), kind=kCustom, calls=%fused_computation.clone.clone.1 | custom fusion | bytes 33558528 | tf_op jit(solution)/shard_map/while/body/eval_jaxpr/while/body/eval_jaxpr/jit(_take)/gather | solution.py:69
  601.2 14.9 %gather_fusion = bf16[1024,32,256]{2,1,0:T(8,128)(2,1)} fusion(bf16[324,32,256]{2,1,0:T(8,128)(2,1)} %get-tuple-element.835, s32[1024]{0:T(1024)S(1)} %broadcast_clamp_fusion.4), kind=kCustom, calls=%fused_computation.clone.clone.1 | custom fusion | bytes 33558528 | tf_op jit(solution)/shard_map/while/body/eval_jaxpr/while/body/eval_jaxpr/jit(_take)/gather | solution.py:69
  638.3 14.9 %gather_fusion = bf16[1024,32,256]{2,1,0:T(8,128)(2,1)} fusion(bf16[324,32,256]{2,1,0:T(8,128)(2,1)} %get-tuple-element.835, s32[1024]{0:T(1024)S(1)} %broadcast_clamp_fusion.4), kind=kCustom, calls=%fused_computation.clone.clone.1 | custom fusion | bytes 33558528 | tf_op jit(solution)/shard_map/while/body/eval_jaxpr/while/body/eval_jaxpr/jit(_take)/gather | solution.py:69
  (322 shorter events, 334.9 us)
Async XLA Ops:
  0.0 28.7 %copy-start = (f32[324,324]{1,0:T(8,128)S(1)}, f32[324,324]{1,0:T(8,128)}, u32[]{:S(2)}) copy-start(f32[324,324]{1,0:T(8,128)} %param.14) | copy-start | bytes 1259716
  17.7 11.1 %copy-start.1 = (f32[32,256]{1,0:T(8,128)S(1)}, f32[32,256]{1,0:T(8,128)}, u32[]{:S(2)}) copy-start(f32[32,256]{1,0:T(8,128)} %param.16) | copy-start | bytes 98308
  17.7 11.0 %copy-start.2 = (s32[32,256]{1,0:T(8,128)S(1)}, s32[32,256]{1,0:T(8,128)}, u32[]{:S(2)}) copy-start(s32[32,256]{1,0:T(8,128)} %param.15) | copy-start | bytes 98308
  19.8 36.8 %all-to-all-start = ((bf16[16,2,128,256]{3,2,1,0:T(8,128)(2,1)}), bf16[16,2,128,256]{3,2,1,0:T(8,128)(2,1)S(1)}, u32[]{:S(2)}, u32[]{:S(2)}) async-start(bf16[16,2,128,256]{3,2,1,0:T(8,128)(2,1)} %copy.31), calls=%async_computation | async-start | bytes 4194304 | tf_op jit(solution)/shard_map/all_to_all | solution.py:30
where the time goes:
time: 673 us; the launch traced here: 669 us
  local copies, waits for them, and re-layouts  355 us (53%)
  matrix products  192 us (29%)
  loops' own time  55.7 us (8%)
  other arithmetic  29.7 us (4%)
  blocking collectives  14.7 us (2%)
  waiting for transfers between devices  14.1 us (2%)
  starting transfers between devices  7.6 us (1%)
    gather x16, local copies, waits for them, and re-layouts, per_pair(): coupled_rows = jnp.take(coupled, orbital_pair, axis=0)  239 us
    dot_general x16, matrix products, per_pair(): jnp.einsum('lbj,lj->lb', coupled_rows, amp_rows, preferred_element_type=j...  167 us
    gather x16, local copies, waits for them, and re-layouts, per_pair(): amp_rows = jnp.take(block, source_row, axis=0)  63.1 us
    another operation x4, loops' own time, per_target(): lax.scan(per_pair, start, jnp.arange(chosen.shape[0], dtype=jnp.int32))  55.7 us
    all_gather x1, blocking collectives, body(): full_rows = lax.all_gather(local_amp, 'beta', axis=2, tiled=True)  14.7 us
    all_to_all x1, waiting for transfers between devices, assemble(): lax.all_to_all(outgoing, 'alpha', split_axis=0, concat_axis=0, tiled=True)  14.1 us
    dot_general x16, matrix products, per_pair(): jnp.dot(hot_rows.T, picked * weights[:, None], precision=lax.Precision.HI...  14 us
    select_n x16, other arithmetic, per_pair(): block = jnp.take(gathered, chosen[pair_index], axis=0)  13.6 us
  transfers between devices with their start and end apart: 1, of which 1 were waited for; matrix products, arithmetic and copies ran while one was open for 2% of the time, Pallas kernels for 0%

commit v1 on v0

v1 whole, which is shorter than its diff:
```python
import functools

import jax
import jax.numpy as jnp
from jax import lax
from jax.experimental import pallas as pl
from jax.experimental.pallas import tpu as pltpu
from jax.sharding import PartitionSpec as P

NP = 324
ABLK = 128
LINKS = 1024
PAIRS = 4
BLK = 4
NB = 256
HALF = 128
QUART = 81
KROWS = 88
KHI = NP - 256
KHIP = 80
CAP = 32
GROUPS = KROWS // 4
NT = (((1,), (1,)), ((), ()))
f32, bf16, i32 = jnp.float32, jnp.bfloat16, jnp.int32


def dot(a, b):
    return jnp.dot(a, b, preferred_element_type=f32)


def dot_nt(a, b):
    return lax.dot_general(a, b, NT, preferred_element_type=f32)


def iota(shape, dim):
    return lax.broadcasted_iota(i32, shape, dim)


def build_coupled(v_ref, ints_ref, coup):
    lo_ids = iota((256, 256), 0).astype(f32)
    hi_ids = iota((KHIP, 256), 0).astype(f32) + 256.0
    ints_lo = ints_ref[:, :256]
    ints_hi = ints_ref[:, 256 : 256 + KHIP]

    def one(ib, carry):
        v = v_ref[pl.ds(ib, 1), :]
        where_to = jnp.abs(v) - 1.0
        sign = jnp.where(v < 0.0, -1.0, 1.0)
        hot_lo = jnp.where(lo_ids == where_to, sign, 0.0).astype(bf16)
        hot_hi = jnp.where(hi_ids == where_to, sign, 0.0).astype(bf16)
        out = dot(ints_lo, hot_lo) + dot(ints_hi, hot_hi)
        start = pl.multiple_of(ib * KROWS, 8)
        coup[0, pl.ds(start, KROWS), :] = out[:, :128]
        coup[1, pl.ds(start, KROWS), :] = out[:, 128:]
        return carry

    lax.fori_loop(0, HALF, one, 0)


def rank_links(klq, rank):
    tri = (iota((256, 384), 0) <= iota((256, 384), 1)).astype(f32).astype(bf16)
    kl_ids = iota((KROWS, 256), 0).astype(f32)

    def one(p, carry):
        carry = list(carry)
        for c in range(4):
            hots = []
            for t in range(BLK):
                row = klq[pl.ds(t * PAIRS + p, 1), c * 256 : (c + 1) * 256]
                hots.append(kl_ids == row)
            stacked = jnp.concatenate([h.astype(f32).astype(bf16) for h in hots], axis=0)
            cum = dot(stacked, tri)
            for t in range(BLK):
                part = cum[t * KROWS : (t + 1) * KROWS]
                base = jnp.concatenate([carry[t], carry[t]], axis=1)
                mine = jnp.where(hots[t], part[:, :256] + base, 0.0)
                got = jnp.sum(mine, axis=0, keepdims=True) - 1.0
                rank[pl.ds(t * PAIRS + p, 1), c * 256 : (c + 1) * 256] = got
                carry[t] = carry[t] + part[:, 256:]
        return tuple(carry)

    zero = jnp.zeros((KROWS, 128), f32)
    lax.fori_loop(0, PAIRS, one, (zero,) * BLK)


def fill_table(lo, hi, u1, u2, t1, t2):
    lo_ids = iota((128, LINKS), 0).astype(f32)
    hi_ids = iota((32, LINKS), 0).astype(f32)

    def target(t, carry):
        a1 = jnp.zeros((128, 32), f32)
        a2 = jnp.zeros((32, 128), f32)
        for p in range(PAIRS):
            i = t * PAIRS + p
            here = lo_ids == lo[pl.ds(i, 1), :]
            v1 = jnp.where(here, u1[pl.ds(i, 1), :], 0.0).astype(bf16)
            v2 = jnp.where(here, u2[pl.ds(i, 1), :], 0.0).astype(bf16)
            group = (hi_ids == hi[pl.ds(i, 1), :]).astype(f32).astype(bf16)
            a1 = a1 + dot_nt(v1, group)
            a2 = a2 + dot_nt(group, v2)
        t1[t] = jnp.concatenate([a1, jnp.zeros((128, 96), f32)], axis=1)
        t2[t] = a2
        return carry

    lax.fori_loop(0, BLK, target, 0)


def apply_links(at_ref, coup, t1, t2, acc):
    tables = [((128 + iota((128, 128), 1)) * (1 << p)).astype(f32) for p in range(PAIRS)]
    row_ids = iota((128, 256), 0).astype(f32)

    def two(g2, carry):
        picked = []
        for h in range(2):
            g = g2 * 2 + h
            rows = []
            for t in range(BLK):
                code = jnp.take_along_axis(t1[t], jnp.full((128, 128), g, i32), axis=1)
                size = jnp.abs(code)
                sign = jnp.where(code < 0.0, -1.0, 1.0)
                hot = jnp.concatenate(
                    [jnp.where(size == tab, sign, 0.0).astype(bf16) for tab in tables], axis=1
                )
                rows.append(dot_nt(hot, at_ref[t]).astype(bf16))
            for k in range(4):
                mine = jnp.concatenate([r[k * CAP : (k + 1) * CAP] for r in rows], axis=0)
                kl = g * 4 + k
                c = jnp.concatenate(
                    [coup[j, pl.ds(kl, HALF, stride=KROWS), :].astype(bf16) for j in range(2)],
                    axis=1,
                )
                picked.append(dot_nt(mine, c).astype(bf16))
        for t in range(BLK):
            block = jnp.concatenate([q[t * CAP : (t + 1) * CAP] for q in picked], axis=0)
            to = jnp.concatenate(
                [t2[t, pl.ds(g2 * 2, 1), :], t2[t, pl.ds(g2 * 2 + 1, 1), :]], axis=1
            )
            hot = (row_ids == to).astype(f32).astype(bf16)
            acc[t] += dot(hot, block)
        return carry

    lax.fori_loop(0, GROUPS // 2, two, 0)


def kernel(at_ref, v_ref, ints_ref, kl0_ref, col_ref, row_ref, coef_ref, count_ref, out_ref,
           coup, klq, rank, lo, hi, u1, u2, t1, t2):
    build_coupled(v_ref, ints_ref, coup)
    col = col_ref[...]
    kl = (col >> 7) - kl0_ref[0]
    filled = iota((BLK * PAIRS, LINKS), 1) < count_ref[...]
    mine = filled & (kl >= 0) & (kl < QUART)
    kl = jnp.where(mine, kl, -1)
    klq[...] = kl.astype(f32)
    power = (1 << (iota((BLK * PAIRS, LINKS), 0) & 3)).astype(f32)
    u1[...] = coef_ref[...] * (128 + (col & 127)).astype(f32) * power
    u2[...] = row_ref[...].astype(f32)
    rank_links(klq, rank)
    rank[...] = jnp.where(mine, rank[...], -1.0)
    most = jnp.max(rank[...]).astype(i32)
    out_ref[...] = jnp.zeros((BLK, ABLK, HALF), f32)

    def one_round(step, carry):
        kl = klq[...].astype(i32)
        r = rank[...].astype(i32) - step * CAP
        ok = (kl >= 0) & (r >= 0) & (r < CAP)
        lo[...] = jnp.where(ok, (kl & 3) * CAP + r, -1).astype(f32)
        hi[...] = jnp.where(ok, kl >> 2, -1).astype(f32)
        fill_table(lo, hi, u1, u2, t1, t2)
        apply_links(at_ref, coup, t1, t2, out_ref)
        return carry

    lax.fori_loop(0, (most + CAP) // CAP, one_round, 0)


def body(amplitudes, integrals, beta_pair, beta_coef, pair_src, link_row, link_col, link_coef, link_count):
    me_a, me_b = lax.axis_index("alpha"), lax.axis_index("beta")
    groups = [[0, 1, 2, 3], [4, 5, 6, 7]]
    own = jnp.transpose(amplitudes.reshape(BLK, ABLK, 32), (0, 2, 1))
    every = lax.all_gather(own, "alpha", axis=0, tiled=True)
    src = lax.dynamic_slice_in_dim(pair_src, me_a * BLK, BLK, 0)
    chosen = jnp.take(every, src.reshape(-1), axis=0).reshape(BLK, PAIRS, 32, ABLK)
    chosen = jnp.transpose(chosen, (0, 2, 1, 3)).reshape(BLK, 32, PAIRS * ABLK)
    at = lax.all_gather(chosen, "beta", axis=1, tiled=True)
    code = beta_coef * (beta_pair + 1).astype(f32)
    v = lax.all_gather(code, "beta", axis=0, tiled=True, axis_index_groups=groups)
    kl0 = (me_b % 4) * QUART
    ints = lax.dynamic_slice_in_dim(integrals, kl0, QUART, 0).astype(bf16)
    ints = jnp.pad(ints, ((0, KROWS - QUART), (0, 384 - NP)))
    vm = pl.BlockSpec(memory_space=pltpu.VMEM)
    part = pl.pallas_call(
        kernel,
        out_shape=jax.ShapeDtypeStruct((BLK, ABLK, HALF), f32),
        in_specs=[vm, vm, vm, pl.BlockSpec(memory_space=pltpu.SMEM), vm, vm, vm, vm],
        out_specs=vm,
        scratch_shapes=[
            pltpu.VMEM((2, HALF * KROWS, 128), f32),
        ] + [pltpu.VMEM((BLK * PAIRS, LINKS), f32)] * 6 + [
            pltpu.VMEM((BLK, 128, 128), f32),
            pltpu.VMEM((BLK, 32, 128), f32),
        ],
        compiler_params=pltpu.CompilerParams(vmem_limit_bytes=48 << 20),
        name="links",
    )(at, v, ints, kl0.reshape(1), link_col.reshape(16, LINKS), link_row.reshape(16, LINKS),
      link_coef.reshape(16, LINKS), link_count.reshape(16, 1))
    part = part.reshape(BLK * ABLK, HALF)
    return lax.psum_scatter(part, "beta", scatter_dimension=1, tiled=True, axis_index_groups=groups)


def solution(mesh):
    in_specs = (P("alpha", "beta"), P(), P("beta", None), P("beta", None), P(),
                P("alpha", None, None), P("alpha", None, None), P("alpha", None, None), P("alpha", None))
    return jax.shard_map(body, mesh=mesh, in_specs=in_specs, out_specs=P("alpha", "beta"), check_vma=False)
```

time: 673 us -> 127 us (0.19)
  local copies, waits for them, and re-layouts: 355 us -> 6.18 us
  matrix products: 192 us -> 0 us
  loops' own time: 55.7 us -> 0 us
  Pallas kernels: 0 us -> 42 us
  other arithmetic: 29.7 us -> 1.59 us
  blocking collectives: 14.7 us -> 32.1 us
  waiting for transfers between devices: 14.1 us -> 31.5 us
  between operations: 0.09 us -> 13.5 us
  starting transfers between devices: 7.6 us -> 0.04 us
    gather x34 -> x1, local copies, waits for them, and re-layouts: 303 us -> 0.58 us  [body(): jnp.take(every, src.reshape(-1), axis=0).reshape(BLK, PAIRS, 32, ABLK)]
    dot_general x34 -> x0, matrix products: 192 us -> none  [the longest x16 167 us: per_pair(): jnp.einsum('lbj,lj->lb', coupled_rows, amp_rows, preferred_element_type=j...]
    another operation x5 -> x0, loops' own time: 55.7 us -> none  [the longest x4 55.7 us: per_target(): lax.scan(per_pair, start, jnp.arange(chosen.shape[0], dtype=jnp.int32))]
    pallas_call x0 -> x1, Pallas kernels: none -> 42 us  [body(): pl.pallas_call(kernel, out_shape=jax.ShapeDtypeStruct((BLK, ABLK, HALF),...]
    dynamic_slice x80 -> x1, local copies, waits for them, and re-layouts: 28.2 us -> 0.09 us  [body(): src = lax.dynamic_slice_in_dim(pair_src, me_a * BLK, BLK, 0)]
    select_n x81 -> x1, other arithmetic: 27.2 us -> 0.01 us  [body(): jnp.take(every, src.reshape(-1), axis=0).reshape(BLK, PAIRS, 32, ABLK)]
    all_gather x1 -> x2, blocking collectives: 14.7 us -> 32.1 us  [the longest x1 21 us: body(): every = lax.all_gather(own, 'alpha', axis=0, tiled=True)]
    reduce_scatter x0 -> x1, waiting for transfers between devices: none -> 17.3 us  [body(): lax.psum_scatter(part, 'beta', scatter_dimension=1, tiled=True, axis_inde...]
  transfers between devices with their start and end apart: 1 -> 2, of which waited for: 1 -> 2; matrix products, arithmetic and copies ran while one was open for 2% -> 0% of each run, Pallas kernels for 0% -> 0%
where the time goes in v1:
time: 127 us
  Pallas kernels  42 us (33%)
  blocking collectives  32.1 us (25%)
  waiting for transfers between devices  31.5 us (25%)
  between operations  13.5 us (11%)
  local copies, waits for them, and re-layouts  6.18 us (5%)
  other arithmetic  1.59 us (1%)
    pallas_call x1, Pallas kernels, body(): pl.pallas_call(kernel, out_shape=jax.ShapeDtypeStruct((BLK, ABLK, HALF),...  42 us
    all_gather x1, blocking collectives, body(): every = lax.all_gather(own, 'alpha', axis=0, tiled=True)  21 us
    reduce_scatter x1, waiting for transfers between devices, body(): lax.psum_scatter(part, 'beta', scatter_dimension=1, tiled=True, axis_inde...  17.3 us
    all_gather x1, waiting for transfers between devices, body(): at = lax.all_gather(chosen, 'beta', axis=1, tiled=True)  14.1 us
    all_gather x1, blocking collectives, body(): lax.all_gather(code, 'beta', axis=0, tiled=True, axis_index_groups=groups)  11.1 us
    unnamed x18, local copies, waits for them, and re-layouts  4.28 us
  transfers between devices with their start and end apart: 2, of which 2 were waited for; matrix products, arithmetic and copies ran while one was open for 0% of the time, Pallas kernels for 0%

profile of v1, /device:TPU:1, one launch (start us, length us, event | category | flops | bytes accessed | tf_op | source)
XLA Modules:
  0.0 127.0 jit_solution(3983729925505719433)
XLA Ops:
  6.5 0.8 compare_and_fusion
  7.4 0.1 copy.25
  7.5 0.1 copy.27
  7.6 0.1 reshape.65
  7.7 21.0 %all_gather.9 = bf16[64,32,128]{2,1,0:T(8,128)(2,1)S(1)} all-gather(bf16[4,32,128]{2,1,0:T(8,128)(2,1)S(1)} %copy.26), channel_id=1, replica_groups=mesh['alpha'=16,'beta'=8] {'alpha'}, dimensions={0}, use_global_device_ids=true | all-gather | bytes 557056 | tf_op jit(solution)/shard_map/all_gather | solution.py:179
  28.7 0.6 gather_fusion
  29.3 0.7 copy_bitcast_fusion
  30.0 0.0 all-gather.2.cloned.1.call-update
  30.0 0.0 reduce-scatter.2.cloned.1.call-start
  30.1 0.7 copy-done.8
  30.8 0.1 reshape.81.count_ref
  30.9 0.8 copy-done.3
  31.7 0.8 copy-done.4
  32.6 0.0 copy-start.5
  32.6 0.0 copy-start.6
  32.7 0.7 copy-done.5
  33.4 0.0 copy-done.6
  33.4 11.1 %all_gather.11.v_ref = f32[128,256]{1,0:T(8,128)S(1)} all-gather(f32[32,256]{1,0:T(8,128)S(1)} %convert_multiply_fusion), channel_id=1, replica_groups={{0,1,2,3},{4,5,6,7},{8,9,10,11},{12,13,14,15},{16,17,18,19},{20,21,22,2..., dimensions={0}, use_global_device_ids=true | all-gather | bytes 163840 | tf_op jit(solution)/shard_map/all_gather | solution.py:185
  44.5 14.1 %all-gather.2.cloned.1.call-done.at_ref = bf16[4,256,512]{2,1,0:T(8,128)(2,1)} async-done(((bf16[4,32,512]{2,1,0:T(8,128)(2,1)}), bf16[4,256,512]{2,1,0:T(8,128)(2,1)}) %all-gather.2.cloned.1.call-update) | async-done | bytes 1048592 | tf_op jit(solution)/shard_map/all_gather | solution.py:183
  58.7 1.2 copy-done.1
  59.9 42.0 %links.1 = f32[4,128,128]{2,1,0:T(8,128)S(1)} custom-call(bf16[4,256,512]{2,1,0:T(8,128)(2,1)S(1)} %copy-done.1, f32[128,256]{1,0:T(8,128)S(1)} %all_gather.11.v_ref, bf16[88,384]{1,0:T(8,128)(2,1)S(1)} %pad.4.ints_ref, s32[1]{0:T(128)} %bitcast.4.kl0_ref, s32[16,1024]{1,0:T(8,128)S(1)} %reshape.68.col_ref, s32[16,1024]{1,0:T(8,128)S(1)} %reshape.69.row_ref, ...), custom_call_target="tpu_custom_call" | custom-call | tf_op jit(solution)/shard_map/links/pallas_call | solution.py:190
  101.9 0.8 copy.30
  102.8 0.0 reduce-scatter.2.cloned.1.call-update
  102.8 17.3 %reduce-scatter.2.cloned.1.call-done = f32[512,32]{0,1:T(8,128)} async-done(((f32[512,128]{0,1:T(8,128)}), f32[512,32]{0,1:T(8,128)}) %reduce-scatter.2.cloned.1.call-update) | async-done | bytes 65552 | tf_op jit(solution)/shard_map/reduce_scatter | solution.py:206
  (21 shorter events, 0.2 us)
Async XLA Ops:
  6.5 26.1 %copy-start = (f32[324,324]{1,0:T(8,128)S(1)}, f32[324,324]{1,0:T(8,128)}, u32[]{:S(2)}) copy-start(f32[324,324]{1,0:T(8,128)} %param.10) | copy-start | bytes 1259716
  6.5 1.1 copy-start.7
  6.5 52.1 %all-gather.2.cloned.1.call-start = ((), (), s32[]{:S(2)}) async-start(), calls=%async_computation.1 | async-start | bytes 1179648 | tf_op jit(solution)/shard_map/all_gather | solution.py:183
  30.0 0.9 copy-start.2
  30.0 90.1 %reduce-scatter.2.cloned.1.call-start = ((), (), s32[]{:S(2)}) async-start(), calls=%async_computation.2 | async-start | bytes 327680 | tf_op jit(solution)/shard_map/reduce_scatter | solution.py:206
  30.1 0.7 copy-start.8
  30.9 0.8 copy-start.3
  31.7 0.8 copy-start.4
  32.6 0.8 copy-start.5
  32.6 0.8 copy-start.6
  58.7 1.2 copy-start.1
Sparse Core Ops, SparseCore 0:
  30.2 28.4 all-gather.1
  102.9 17.1 reduce-scatter.1

commit v2 on v1

v2 whole, which is shorter than its diff:
```python
import jax
import jax.numpy as jnp
from jax import lax
from jax.experimental import pallas as pl
from jax.experimental.pallas import tpu as pltpu
from jax.sharding import PartitionSpec as P

NP = 324
ABLK = 128
LINKS = 1024
PAIRS = 4
BLK = 4
NB = 256
SLAB = 32
ALPHA = 16
HALF = 128
QUART = 81
KROWS = 88
KHIP = 80
CAP = 32
GROUPS = 21
GCHUNK = 7
NTDIMS = (((1,), (1,)), ((), ()))
f32, bf16, i32 = jnp.float32, jnp.bfloat16, jnp.int32
MESH = pl.DeviceIdType.MESH


def dot(a, b):
    return jnp.dot(a, b, preferred_element_type=f32)


def dot_nt(a, b):
    return lax.dot_general(a, b, NTDIMS, preferred_element_type=f32)


def iota(shape, dim):
    return lax.broadcasted_iota(i32, shape, dim)


def hot_bf16(mask):
    return mask.astype(f32).astype(bf16)


def my_integrals(integ, first):
    rows = hot_bf16(iota((KROWS, NP), 1) - first == iota((KROWS, NP), 0))
    rows = jnp.where(iota((KROWS, NP), 0) < QUART, rows, jnp.zeros((), bf16))
    mine = dot(rows, integ[...].astype(bf16)).astype(bf16)
    shift = hot_bf16(iota((NP, 128), 0) - 256 == iota((NP, 128), 1))
    return mine[:, :256], dot(mine, shift).astype(bf16)[:, :KHIP]


def build_coupled(v_ref, ints, coup, begin, end):
    lo_ids = iota((256, 256), 0).astype(f32)
    hi_ids = iota((KHIP, 256), 0).astype(f32) + 256.0
    ints_lo, ints_hi = ints

    def one(ib, carry):
        v = v_ref[pl.ds(ib, 1), :]
        where_to = jnp.abs(v) - 1.0
        sign = jnp.where(v < 0.0, -1.0, 1.0)
        hot_lo = jnp.where(lo_ids == where_to, sign, 0.0).astype(bf16)
        hot_hi = jnp.where(hi_ids == where_to, sign, 0.0).astype(bf16)
        out = dot(ints_lo, hot_lo) + dot(ints_hi, hot_hi)
        start = pl.multiple_of(ib * KROWS, 8)
        coup[0, pl.ds(start, KROWS), :] = out[:, :128]
        coup[1, pl.ds(start, KROWS), :] = out[:, 128:]
        return carry

    lax.fori_loop(begin, end, one, 0, unroll=16)


def rank_links(klq, rank):
    tri = hot_bf16(iota((256, 384), 0) <= iota((256, 384), 1))
    kl_ids = iota((KROWS, 256), 0).astype(f32)

    def one(p, carry):
        carry = list(carry)
        for c in range(4):
            hots = []
            for t in range(BLK):
                row = klq[pl.ds(t * PAIRS + p, 1), c * 256 : (c + 1) * 256]
                hots.append(kl_ids == row)
            stacked = jnp.concatenate([hot_bf16(h) for h in hots], axis=0)
            cum = dot(stacked, tri)
            for t in range(BLK):
                part = cum[t * KROWS : (t + 1) * KROWS]
                base = jnp.concatenate([carry[t], carry[t]], axis=1)
                mine = jnp.where(hots[t], part[:, :256] + base, 0.0)
                got = jnp.sum(mine, axis=0, keepdims=True) - 1.0
                rank[pl.ds(t * PAIRS + p, 1), c * 256 : (c + 1) * 256] = got
                carry[t] = carry[t] + part[:, 256:]
        return tuple(carry)

    zero = jnp.zeros((KROWS, 128), f32)
    lax.fori_loop(0, PAIRS, one, (zero,) * BLK)


def fill_tables(lo, hi, u1, u2, t1, t2):
    lo_ids = iota((128, LINKS), 0).astype(f32)
    hi_ids = iota((32, LINKS), 0).astype(f32)

    def target(t, carry):
        a1 = jnp.zeros((128, 32), f32)
        a2 = jnp.zeros((32, 128), f32)
        for p in range(PAIRS):
            i = t * PAIRS + p
            here = lo_ids == lo[pl.ds(i, 1), :]
            v1 = jnp.where(here, u1[pl.ds(i, 1), :], 0.0).astype(bf16)
            v2 = jnp.where(here, u2[pl.ds(i, 1), :], 0.0).astype(bf16)
            group = hot_bf16(hi_ids == hi[pl.ds(i, 1), :])
            a1 = a1 + dot_nt(v1, group)
            a2 = a2 + dot_nt(group, v2)
        t1[t] = jnp.concatenate([a1, jnp.zeros((128, 96), f32)], axis=1)
        t2[t] = a2
        return carry

    lax.fori_loop(0, BLK, target, 0)


def gather_rows(at, t1, gs):
    tables = [((128 + iota((128, 128), 1)) * (1 << p)).astype(f32) for p in range(PAIRS)]

    def one(c, carry):
        for t in range(BLK):
            hots = []
            for h in range(GCHUNK):
                code = jnp.take_along_axis(t1[t], jnp.full((128, 128), c * GCHUNK + h, i32), axis=1)
                size = jnp.abs(code)
                sign = jnp.where(code < 0.0, -1.0, 1.0)
                hots.append(
                    jnp.concatenate(
                        [jnp.where(size == tab, sign, 0.0).astype(bf16) for tab in tables], axis=1
                    )
                )
            amps = at[:, t].reshape(NB, PAIRS * ABLK)
            rows = dot_nt(jnp.concatenate(hots, axis=0), amps).astype(bf16)
            for h in range(GCHUNK):
                for k in range(4):
                    s = h * 128 + k * CAP
                    gs[(c * GCHUNK + h) * 4 + k, t * CAP : (t + 1) * CAP, :] = rows[s : s + CAP]
        return carry

    lax.fori_loop(0, GROUPS // GCHUNK, one, 0)


def pick(coup, gs, ps):
    def one(kl, carry):
        c = jnp.concatenate(
            [coup[j, pl.ds(kl, HALF, stride=KROWS), :].astype(bf16) for j in range(2)], axis=1
        )
        q = dot_nt(gs[kl], c).astype(bf16)
        start = pl.multiple_of(kl * CAP, CAP)
        for t in range(BLK):
            ps[t, pl.ds(start, CAP), :] = q[t * CAP : (t + 1) * CAP]
        return carry

    lax.fori_loop(0, QUART, one, 0, unroll=27)
    for t in range(BLK):
        ps[t, QUART * CAP :, :] = jnp.zeros((4 * CAP * GROUPS - QUART * CAP, HALF), bf16)


def add_rows(t2, ps, t):
    ids = iota((128, 128), 0).astype(f32)
    hot = jnp.concatenate([hot_bf16(ids == t2[t, g : g + 1, :]) for g in range(GROUPS)], axis=1)
    return dot(hot, ps[t])


def kernel(amp_h, integ_h, pair_h, coef_h, src, col_h, row_h, lcoef_h, count, out, at_out, flag_out,
           amp, integ, pair, coef, col, row, lcoef, own, ev, vall, at, coup, klq, rank, lo, hi, u1, u2,
           t1, t2, gs, ps, sb, rb, fl, in_sem, a_send, a_recv, v_send, v_recv, y_send, y_recv, s_send,
           s_recv, r_send, r_recv, f_send, f_recv, o_sem):
    a, b = lax.axis_index("alpha"), lax.axis_index("beta")
    y, core = b // 2, b % 2
    first, q = b // 4 * 4, b % 4
    sibling = y * 2 + 1 - core
    mates = [first + (q + k) % 4 for k in range(1, 4)]
    rings = [(y + k) % 4 * 2 + core for k in range(1, 4)]
    back = [(y + 4 - k) % 4 * 2 + core for k in range(1, 4)]

    loads = []
    for n, (h, m) in enumerate([(amp_h, amp), (pair_h, pair), (coef_h, coef), (col_h, col), (row_h, row),
                                (lcoef_h, lcoef), (integ_h, integ)]):
        loads.append(pltpu.make_async_copy(h, m, in_sem.at[n]))
        loads[-1].start()

    barrier = pltpu.get_barrier_semaphore()
    for k in range(1, ALPHA):
        pl.semaphore_signal(barrier, inc=1, device_id=((a + k) % ALPHA, b), device_id_type=MESH)
    for k in range(1, 8):
        pl.semaphore_signal(barrier, inc=1, device_id=(a, (b + k) % 8), device_id_type=MESH)

    loads[0].wait()
    eye = hot_bf16(iota((SLAB, SLAB), 0) == iota((SLAB, SLAB), 1))
    for j in range(BLK):
        own[j] = dot_nt(eye, amp[j * ABLK : (j + 1) * ABLK, :]).astype(bf16)
    loads[1].wait()
    loads[2].wait()
    mine = pl.ds(pl.multiple_of(q * SLAB, SLAB), SLAB)
    vall[mine, :] = coef[...] * (pair[...] + 1).astype(f32)
    pl.semaphore_wait(barrier, ALPHA - 1 + 7)

    def remote(source, target, send, recv, to):
        c = pltpu.make_async_remote_copy(src_ref=source, dst_ref=target, send_sem=send, recv_sem=recv,
                                         device_id=to, device_id_type=MESH)
        c.start()
        return c

    ev[pl.ds(a * BLK, BLK)] = own[...]
    a_copies = [
        remote(own, ev.at[pl.ds(a * BLK, BLK)], a_send.at[k - 1], a_recv.at[k - 1], ((a + k) % ALPHA, b))
        for k in range(1, ALPHA)
    ]
    v_copies = [
        remote(vall.at[mine], vall.at[mine], v_send.at[k], v_recv.at[k], (a, m)) for k, m in enumerate(mates)
    ]

    for n in (3, 4, 5):
        loads[n].wait()
    for t in range(BLK):
        column = col[t]
        kl = (column >> 7) - q * QUART
        slot = iota((PAIRS, LINKS), 1)
        part = iota((PAIRS, LINKS), 0)
        full = jnp.zeros((PAIRS, LINKS), i32)
        for p in range(PAIRS):
            full = jnp.where(part == p, count[t, p], full)
        kl = jnp.where((slot < full) & (kl >= 0) & (kl < QUART), kl, -1)
        at_rows = slice(t * PAIRS, (t + 1) * PAIRS)
        klq[at_rows, :] = kl.astype(f32)
        u1[at_rows, :] = lcoef[t] * ((128 + (column & 127)) << part).astype(f32)
        u2[at_rows, :] = row[t].astype(f32)
    rank_links(klq, rank)
    kl = klq[...].astype(i32)
    r = rank[...].astype(i32)
    ok = (kl >= 0) & (r < CAP)
    lo[...] = jnp.where(ok, (kl & 3) * CAP + r, -1).astype(f32)
    hi[...] = jnp.where(ok, kl >> 2, -1).astype(f32)
    fl[q] = jnp.broadcast_to(jnp.max(rank[...], keepdims=True), (8, 128))
    f_copies = [
        remote(fl.at[q], fl.at[q], f_send.at[k], f_recv.at[k], (a, m)) for k, m in enumerate(mates)
    ]
    fill_tables(lo, hi, u1, u2, t1, t2)

    for c in a_copies:
        c.wait_recv()
    for t in range(BLK):
        for p in range(PAIRS):
            at[b, t, :, p * ABLK : (p + 1) * ABLK] = ev[src[a * BLK + t, p]]
    y_copies = [
        remote(at.at[b], at.at[b], y_send.at[k], y_recv.at[k], (a, m)) for k, m in enumerate(rings)
    ]
    s_copies = [remote(at.at[b], at.at[b], s_send.at[3], s_recv.at[3], (a, sibling))]

    for c in v_copies:
        c.wait_recv()
    loads[6].wait()
    ints = my_integrals(integ, q * QUART)
    build_coupled(vall, ints, coup, 0, 80)
    for k in (0, 2, 1):
        y_copies[k].wait_recv()
        s_copies.append(
            remote(at.at[back[k]], at.at[back[k]], s_send.at[k], s_recv.at[k], (a, sibling))
        )
    build_coupled(vall, ints, coup, 80, HALF)
    for c in s_copies:
        c.wait_recv()
    keep = pltpu.make_async_copy(at, at_out, o_sem)
    keep.start()

    gather_rows(at, t1, gs)
    pick(coup, gs, ps)
    sums = []
    for t in range(BLK):
        sums.append(add_rows(t2, ps, t).T)
    for k in range(4):
        sb[k] = jnp.concatenate([s[k * SLAB : (k + 1) * SLAB] for s in sums], axis=1)
    for k in range(4):
        rb[4 + k] = sb[k].astype(bf16)
    r_copies = [
        remote(rb.at[4 + (q + k) % 4], rb.at[q], r_send.at[k - 1], r_recv.at[k - 1], (a, mates[k - 1]))
        for k in range(1, 4)
    ]
    total = sb[q]
    for k in range(1, 4):
        r_copies[k - 1].wait_recv()
        total = total + rb[(q + 4 - k) % 4].astype(f32)
    for t in range(BLK):
        out[t * ABLK : (t + 1) * ABLK, :] = total[:, t * ABLK : (t + 1) * ABLK].T
    for c in f_copies:
        c.wait_recv()
    flag_out[...] = jnp.maximum(jnp.maximum(fl[0], fl[1]), jnp.maximum(fl[2], fl[3]))
    keep.wait()
    for c in a_copies + v_copies + f_copies + y_copies + s_copies + r_copies:
        c.wait_send()


def by_links(at, integrals, beta_pair, beta_coef, link_row, link_col, link_coef, link_count):
    blocks = at.transpose(1, 3, 0, 2).reshape(BLK, PAIRS * ABLK, NB)
    pair_hot = (beta_pair[None] == jnp.arange(NP, dtype=i32)[:, None, None]).astype(f32)
    looked_up = jnp.einsum("ki,ibj->kbj", integrals, pair_hot, precision=lax.Precision.HIGHEST)
    coupled = (looked_up * beta_coef[None]).astype(bf16)
    slots = jnp.arange(LINKS, dtype=i32)

    def one(sigma, index):
        t, p = index // PAIRS, index % PAIRS
        column = link_col[t, p]
        amps = jnp.take(blocks[t], p * ABLK + column % ABLK, axis=0)
        rows = jnp.take(coupled, column // ABLK, axis=0)
        picked = jnp.einsum("lbj,lj->lb", rows, amps, preferred_element_type=f32)
        weights = jnp.where(slots < link_count[t, p], link_coef[t, p], 0.0)
        return sigma.at[t * ABLK + link_row[t, p]].add(picked * weights[:, None]), None

    sigma = jnp.zeros((BLK * ABLK, SLAB), f32)
    return lax.scan(one, sigma, jnp.arange(BLK * PAIRS, dtype=i32))[0]


def body(amplitudes, integrals, beta_pair, beta_coef, pair_src, link_row, link_col, link_coef, link_count):
    anym = pl.BlockSpec(memory_space=pl.ANY)
    smem = pl.BlockSpec(memory_space=pltpu.SMEM)
    vmem = pl.BlockSpec(memory_space=pltpu.VMEM)
    rows = pltpu.VMEM((BLK * PAIRS, LINKS), f32)
    dma = pltpu.SemaphoreType.DMA
    sigma, at, most = pl.pallas_call(
        kernel,
        out_shape=(
            jax.ShapeDtypeStruct((BLK * ABLK, SLAB), f32),
            jax.ShapeDtypeStruct((8, BLK, SLAB, PAIRS * ABLK), bf16),
            jax.ShapeDtypeStruct((8, 128), f32),
        ),
        in_specs=[anym, anym, anym, anym, smem, anym, anym, anym, smem],
        out_specs=(vmem, anym, vmem),
        scratch_shapes=[
            pltpu.VMEM((BLK * ABLK, SLAB), bf16),
            pltpu.VMEM((NP, NP), f32),
            pltpu.VMEM((SLAB, NB), i32),
            pltpu.VMEM((SLAB, NB), f32),
            pltpu.VMEM((BLK, PAIRS, LINKS), i32),
            pltpu.VMEM((BLK, PAIRS, LINKS), i32),
            pltpu.VMEM((BLK, PAIRS, LINKS), f32),
            pltpu.VMEM((BLK, SLAB, ABLK), bf16),
            pltpu.VMEM((ALPHA * BLK, SLAB, ABLK), bf16),
            pltpu.VMEM((HALF, NB), f32),
            pltpu.VMEM((8, BLK, SLAB, PAIRS * ABLK), bf16),
            pltpu.VMEM((2, HALF * KROWS, 128), f32),
            rows, rows, rows, rows, rows, rows,
            pltpu.VMEM((BLK, 128, 128), f32),
            pltpu.VMEM((BLK, 32, 128), f32),
            pltpu.VMEM((GROUPS * 4, BLK * CAP, NB), bf16),
            pltpu.VMEM((BLK, GROUPS * 4 * CAP, HALF), bf16),
            pltpu.VMEM((4, SLAB, BLK * ABLK), f32),
            pltpu.VMEM((8, SLAB, BLK * ABLK), bf16),
            pltpu.VMEM((4, 8, 128), f32),
            dma((7,)), dma((15,)), dma((15,)), dma((3,)), dma((3,)), dma((3,)), dma((3,)), dma((4,)),
            dma((4,)), dma((3,)), dma((3,)), dma((3,)), dma((3,)), dma,
        ],
        compiler_params=pltpu.CompilerParams(
            vmem_limit_bytes=48 << 20, collective_id=0, has_side_effects=True
        ),
        name="sigma_links",
    )(amplitudes, integrals, beta_pair, beta_coef, pair_src, link_col, link_row, link_coef, link_count)
    return lax.cond(
        jnp.max(most) >= CAP,
        lambda: by_links(at, integrals, beta_pair, beta_coef, link_row, link_col, link_coef, link_count),
        lambda: sigma,
    )


def solution(mesh):
    in_specs = (P("alpha", "beta"), P(), P("beta", None), P("beta", None), P(),
                P("alpha", None, None), P("alpha", None, None), P("alpha", None, None), P("alpha", None))
    return jax.shard_map(body, mesh=mesh, in_specs=in_specs, out_specs=P("alpha", "beta"), check_vma=False)
```

time: 127 us -> 43 us (0.34)
  blocking collectives: 32.1 us -> 0 us
  waiting for transfers between devices: 31.5 us -> 0 us
  between operations: 13.5 us -> 0.67 us
  Pallas kernels: 42 us -> 37.5 us
  local copies, waits for them, and re-layouts: 6.18 us -> 3.34 us
    all_gather x2 -> x0, blocking collectives: 32.1 us -> none  [the longest x1 21 us: body(): every = lax.all_gather(own, 'alpha', axis=0, tiled=True)]
    reduce_scatter x1 -> x0, waiting for transfers between devices: 17.3 us -> none  [body(): lax.psum_scatter(part, 'beta', scatter_dimension=1, tiled=True, axis_inde...]
    all_gather x1 -> x0, waiting for transfers between devices: 14.1 us -> none  [body(): at = lax.all_gather(chosen, 'beta', axis=1, tiled=True)]
    pallas_call x1, Pallas kernels: 42 us -> 37.5 us  [body(): pl.pallas_call(kernel, out_shape=(jax.ShapeDtypeStruct((BLK * ABLK, SLAB)...]
    unnamed x18 -> x3, local copies, waits for them, and re-layouts: 4.28 us -> 3.34 us
  transfers between devices with their start and end apart: 2 -> 0, of which waited for: 2 -> 0; matrix products, arithmetic and copies ran while one was open for 0% -> 0% of each run, Pallas kernels for 0% -> 0%
where the time goes in v2:
time: 43 us; the launch traced here: 42.3 us
  Pallas kernels  37.5 us (87%)
  local copies, waits for them, and re-layouts  3.34 us (8%)
  between operations  0.67 us (2%)
  other arithmetic  0.6 us (1%)
    pallas_call x1, Pallas kernels, body(): pl.pallas_call(kernel, out_shape=(jax.ShapeDtypeStruct((BLK * ABLK, SLAB)...  37.5 us
    unnamed x3, local copies, waits for them, and re-layouts  3.34 us

profile of v2, /device:TPU:1, one launch (start us, length us, event | category | flops | bytes accessed | tf_op | source)
XLA Modules:
  0.0 42.3 jit_solution(13768707176953682860)
XLA Ops:
  0.0 0.9 %copy.19.amp_h = bf16[512,32]{1,0:T(8,128)(2,1)S(1)} copy(bf16[512,32]{0,1:T(8,128)(2,1)} %param.13) | data formatting | bytes 65536 | tf_op args[0]
  0.9 0.8 %copy.20.src = s32[64,4]{1,0:T(8,128)S(1)} copy(s32[64,4]{0,1:T(4,128)} %param.17) | data formatting | bytes 2048 | tf_op args[4]
  1.7 37.5 %sigma_links.1 = (f32[512,32]{1,0:T(8,128)}, bf16[8,4,32,512]{3,2,1,0:T(8,128)(2,1)S(1)}, f32[8,128]{1,0:T(8,128)S(1)}) custom-call(bf16[512,32]{1,0:T(8,128)(2,1)S(1)} %copy.19.amp_h, f32[324,324]{1,0:T(8,128)} %integ_h.1, s32[32,256]{1,0:T(8,128)} %pair_h.1, f32[32,256]{1,0:T(8,128)} %coef_h.1, s32[64,4]{1,0:T(8,128)S(1)} %copy.20.src, ...), custom_call_target="tpu_custom_call" | custom-call | tf_op jit(solution)/shard_map/sigma_links/pallas_call | solution.py:323
  39.2 0.6 %reduce_max.9 = f32[]{:T(128)} reduce(f32[8,128]{1,0:T(8,128)S(1)} %get-tuple-element.205, f32[]{:T(128)} %constant.170.clone.1), dimensions={0,1}, to_apply=%region_0.0 | reduce | flops 1023 | bytes 4104 | tf_op jit(solution)/shard_map/reduce_max | solution.py:362
  40.4 0.2 conditional.1
  40.7 1.7 %copy.22 = f32[512,32]{0,1:T(8,128)} copy(f32[512,32]{1,0:T(8,128)} %get-tuple-element.208) | data formatting | bytes 131072

commit v3 on v0

--- a/solution.py
+++ b/solution.py
@@ -1,12 +1,334 @@
 import jax
 import jax.numpy as jnp
 from jax import lax
+from jax.experimental import pallas as pl
+from jax.experimental.pallas import tpu as pltpu
 from jax.sharding import PartitionSpec as P
 
 NP = 324
 ABLK = 128
 LINKS = 1024
+PAIRS = 4
+BLK = 4
+NB = 256
+SLAB = 32
+ALPHA = 16
+HALF = 128
+QUART = 81
+KROWS = 88
+KHIP = 80
 FETCH_CAP = 2
+CAP = 32
+GROUPS = 21
+GCHUNK = 7
+NTDIMS = (((1,), (1,)), ((), ()))
+f32, bf16, i32 = jnp.float32, jnp.bfloat16, jnp.int32
+MESH = pl.DeviceIdType.MESH
+
+
+def dot(a, b):
+    return jnp.dot(a, b, preferred_element_type=f32)
+
+
+def dot_nt(a, b):
+    return lax.dot_general(a, b, NTDIMS, preferred_element_type=f32)
+
+
+def iota(shape, dim):
+    return lax.broadcasted_iota(i32, shape, dim)
+
+
+def hot_bf16(mask):
+    return mask.astype(f32).astype(bf16)
+
+
+def wanted(src, device, owner):
+    bits = jnp.int32(0)
+    for t in range(BLK):
+        for p in range(PAIRS):
+            block = src[p, device * BLK + t]
+            bits = bits | jnp.where((block >> 2) == owner, bit_of(block & 3), 0)
+    return bits
+
+
+def bit_of(j):
+    return jnp.where(j == 0, 1, jnp.where(j == 1, 2, jnp.where(j == 2, 4, 8)))
+
+
+def lowest(bits):
+    return jnp.where(
+        (bits & 1) != 0, 0, jnp.where((bits & 2) != 0, 1, jnp.where((bits & 4) != 0, 2, 3))
+    )
+
+
+def my_integrals(integ, first):
+    rows = hot_bf16(iota((KROWS, NP), 1) - first == iota((KROWS, NP), 0))
+    rows = jnp.where(iota((KROWS, NP), 0) < QUART, rows, jnp.zeros((), bf16))
+    mine = dot(rows, integ[...].astype(bf16)).astype(bf16)
+    shift = hot_bf16(iota((NP, 128), 0) - 256 == iota((NP, 128), 1))
+    return mine[:, :256], dot(mine, shift).astype(bf16)[:, :KHIP]
+
+
+def build_coupled(v_ref, ints, coup, begin, end):
+    lo_ids = iota((256, 256), 0).astype(f32)
+    hi_ids = iota((KHIP, 256), 0).astype(f32) + 256.0
+    ints_lo, ints_hi = ints
+
+    def one(i, carry):
+        v = jnp.concatenate([v_ref[pl.ds(i * 2, 1), :], v_ref[pl.ds(i * 2 + 1, 1), :]], axis=1)
+        where_to = jnp.abs(v) - 1.0
+        sign = jnp.where(v < 0.0, -1.0, 1.0)
+        hot_lo = jnp.where(lo_ids == where_to, sign, 0.0).astype(bf16)
+        hot_hi = jnp.where(hi_ids == where_to, sign, 0.0).astype(bf16)
+        out = dot(ints_lo, hot_lo) + dot(ints_hi, hot_hi)
+        for h in range(2):
+            start = pl.multiple_of((i * 2 + h) * KROWS, 8)
+            coup[pl.ds(start, KROWS), :] = out[:, h * HALF : (h + 1) * HALF]
+        return carry
+
+    lax.fori_loop(begin // 2, end // 2, one, 0, unroll=16)
+
+
+def rank_links(klq, rank):
+    tri = hot_bf16(iota((256, 384), 0) <= iota((256, 384), 1))
+    kl_ids = iota((KROWS, 256), 0).astype(f32)
+
+    def one(p, carry):
+        carry = list(carry)
+        for c in range(4):
+            hots = []
+            for t in range(BLK):
+                row = klq[pl.ds(t * PAIRS + p, 1), c * 256 : (c + 1) * 256]
+                hots.append(kl_ids == row)
+            stacked = jnp.concatenate([hot_bf16(h) for h in hots], axis=0)
+            cum = dot(stacked, tri)
+            for t in range(BLK):
+                part = cum[t * KROWS : (t + 1) * KROWS]
+                base = jnp.concatenate([carry[t], carry[t]], axis=1)
+                mine = jnp.where(hots[t], part[:, :256] + base, 0.0)
+                got = jnp.sum(mine, axis=0, keepdims=True) - 1.0
+                rank[pl.ds(t * PAIRS + p, 1), c * 256 : (c + 1) * 256] = got
+                carry[t] = carry[t] + part[:, 256:]
+        return tuple(carry)
+
+    zero = jnp.zeros((KROWS, 128), f32)
+    lax.fori_loop(0, PAIRS, one, (zero,) * BLK)
+
+
+def fill_tables(lo, hi, u1, u2, t1, t2):
+    lo_ids = iota((128, LINKS), 0).astype(f32)
+    hi_ids = iota((32, LINKS), 0).astype(f32)
+
+    def target(t, carry):
+        a1 = jnp.zeros((128, 32), f32)
+        a2 = jnp.zeros((32, 128), f32)
+        for p in range(PAIRS):
+            i = t * PAIRS + p
+            here = lo_ids == lo[pl.ds(i, 1), :]
+            v1 = jnp.where(here, u1[pl.ds(i, 1), :], 0.0).astype(bf16)
+            v2 = jnp.where(here, u2[pl.ds(i, 1), :], 0.0).astype(bf16)
+            group = hot_bf16(hi_ids == hi[pl.ds(i, 1), :])
+            a1 = a1 + dot_nt(v1, group)
+            a2 = a2 + dot_nt(group, v2)
+        t1[t] = jnp.concatenate([a1, jnp.zeros((128, 96), f32)], axis=1)
+        t2[t] = a2
+        return carry
+
+    lax.fori_loop(0, BLK, target, 0)
+
+
+def gather_rows(at, t1, gs, t):
+    tables = [((128 + iota((128, 128), 1)) * (1 << p)).astype(f32) for p in range(PAIRS)]
+    amps = at[:, t].reshape(HALF, PAIRS * ABLK)
+    for c in range(GROUPS // GCHUNK):
+        hots = []
+        for h in range(GCHUNK):
+            code = jnp.take_along_axis(t1[t], jnp.full((128, 128), c * GCHUNK + h, i32), axis=1)
+            size = jnp.abs(code)
+            sign = jnp.where(code < 0.0, -1.0, 1.0)
+            hots.append(
+                jnp.concatenate([jnp.where(size == tab, sign, 0.0).astype(bf16) for tab in tables], axis=1)
+            )
+        rows = dot_nt(jnp.concatenate(hots, axis=0), amps).astype(bf16)
+        for h in range(GCHUNK):
+            for k in range(4):
+                s = h * 128 + k * CAP
+                gs[(c * GCHUNK + h) * 4 + k, t * CAP : (t + 1) * CAP, :] = rows[s : s + CAP]
+
+
+def pick(coup, gs, ps):
+    def one(kl, carry):
+        c = coup[pl.ds(kl, NB, stride=KROWS), :].astype(bf16)
+        q = dot_nt(gs[kl], c).astype(bf16)
+        start = pl.multiple_of(kl * CAP, CAP)
+        for t in range(BLK):
+            ps[t, pl.ds(start, CAP), :] = q[t * CAP : (t + 1) * CAP]
+        return carry
+
+    lax.fori_loop(0, QUART, one, 0, unroll=27)
+    for t in range(BLK):
+        ps[t, QUART * CAP :, :] = jnp.zeros((4 * CAP * GROUPS - QUART * CAP, NB), bf16)
+
+
+def add_rows(t2, ps, t):
+    ids = iota((128, 128), 0).astype(f32)
+    hot = jnp.concatenate([hot_bf16(ids == t2[t, g : g + 1, :]) for g in range(GROUPS)], axis=1)
+    return dot(hot, ps[t])
+
+
+def kernel(amp_h, integ_h, pair_h, coef_h, src_h, col_h, row_h, lcoef_h, count_h, out, flag_out,
+           src, count, amp, blocks, give, integ, pair, coef, col, row, lcoef, ev, vown, vall, at, coup, klq, rank, lo, hi, u1, u2,
+           t1, t2, gs, ps, sb, rb, fl, in_sem, a_send, a_recv, v_send, v_recv, y_send, y_recv, s_send,
+           s_recv, r_send, r_recv, f_send, f_recv, g_send, g_recv):
+    a, b = lax.axis_index("alpha"), lax.axis_index("beta")
+    core = b % 2
+    half, q = b // 4, b % 4
+    x, z = a // 4, a % 4
+    sibling = b // 2 * 2 + 1 - core
+    across = half * 4 + (q + 2) % 4
+    peers = [(b + k) % 8 for k in range(1, 8)]
+
+    loads = []
+    for n, (h, m) in enumerate([(amp_h, amp), (pair_h, pair), (coef_h, coef), (col_h, col), (row_h, row),
+                                (lcoef_h, lcoef), (integ_h, integ), (src_h, src),
+                                (count_h, count)]):
+        loads.append(pltpu.make_async_copy(h, m, in_sem.at[n]))
+        loads[-1].start()
+
+    barrier = pltpu.get_barrier_semaphore()
+    for k in range(1, ALPHA):
+        pl.semaphore_signal(barrier, inc=1, device_id=((a + k) % ALPHA, b), device_id_type=MESH)
+    for k in range(1, 8):
+        pl.semaphore_signal(barrier, inc=1, device_id=(a, (b + k) % 8), device_id_type=MESH)
+
+    loads[0].wait()
+    loads[7].wait()
+    for j in range(BLK):
+        blocks[j] = amp[:, j * ABLK : (j + 1) * ABLK]
+    for k in range(ALPHA):
+        asked = wanted(src, (a + k) % ALPHA, a)
+        low = lowest(asked)
+        for n, j in enumerate((low, lowest(asked - bit_of(low)))):
+            give[k, n] = blocks[j]
+    ev[pl.ds(a * FETCH_CAP, FETCH_CAP)] = give[0]
+    pl.semaphore_wait(barrier, ALPHA - 1 + 7)
+
+    def remote(source, target, send, recv, to):
+        c = pltpu.make_async_remote_copy(src_ref=source, dst_ref=target, send_sem=send, recv_sem=recv,
+                                         device_id=to, device_id_type=MESH)
+        c.start()
+        return c
+
+    a_copies = [
+        remote(give.at[k], ev.at[pl.ds(a * FETCH_CAP, FETCH_CAP)], a_send.at[k - 1], a_recv.at[k - 1], ((a + k) % ALPHA, b))
+        for k in range(1, ALPHA)
+    ]
+    loads[1].wait()
+    loads[2].wait()
+    mine = pl.ds(pl.multiple_of(b * SLAB, SLAB), SLAB)
+    codes = coef[...] * (pair[...] + 1).astype(f32)
+    for h in range(2):
+        vown[h] = codes[:, h * HALF : (h + 1) * HALF]
+    vall[mine, :] = vown[half]
+    v_copies = [
+        remote(vown.at[m // 4], vall.at[mine], v_send.at[k], v_recv.at[k], (a, m)) for k, m in enumerate(peers)
+    ]
+
+    for n in (3, 4, 5, 8):
+        loads[n].wait()
+    for t in range(BLK):
+        column = col[t]
+        kl = (column >> 7) - q * QUART
+        slot = iota((PAIRS, LINKS), 1)
+        part = iota((PAIRS, LINKS), 0)
+        full = jnp.zeros((PAIRS, LINKS), i32)
+        for p in range(PAIRS):
+            full = jnp.where(part == p, count[t, p], full)
+        kl = jnp.where((slot < full) & (kl >= 0) & (kl < QUART), kl, -1)
+        at_rows = slice(t * PAIRS, (t + 1) * PAIRS)
+        klq[at_rows, :] = kl.astype(f32)
+        u1[at_rows, :] = lcoef[t] * ((128 + (column & 127)) << part).astype(f32)
+        u2[at_rows, :] = row[t].astype(f32)
+    rank_links(klq, rank)
+    kl = klq[...].astype(i32)
+    r = rank[...].astype(i32)
+    ok = (kl >= 0) & (r < CAP)
+    lo[...] = jnp.where(ok, (kl & 3) * CAP + r, -1).astype(f32)
+    hi[...] = jnp.where(ok, kl >> 2, -1).astype(f32)
+    fl[b] = jnp.broadcast_to(jnp.max(rank[...], keepdims=True), (8, 128))
+    f_copies = [
+        remote(fl.at[b], fl.at[b], f_send.at[k], f_recv.at[k], (a, m)) for k, m in enumerate(peers)
+    ]
+    fill_tables(lo, hi, u1, u2, t1, t2)
+
+    for c in a_copies:
+        c.wait_recv()
+    y_copies, s_copies = [], []
+    for t in range(BLK):
+        for p in range(PAIRS):
+            block = src[p, a * BLK + t]
+            owner = block >> 2
+            below = wanted(src, a, owner) & (bit_of(block & 3) - 1)
+            at[q, t, :, p * ABLK : (p + 1) * ABLK] = ev[
+                owner * FETCH_CAP + jnp.where(below != 0, 1, 0)
+            ]
+        mine = at.at[q, t]
+        y_copies.append(remote(mine, mine, y_send.at[t], y_recv.at[t], (a, across)))
+        s_copies.append([remote(mine, mine, s_send.at[t, 0], s_recv.at[t, 0], (a, sibling))])
+
+    for c in v_copies:
+        c.wait_recv()
+    loads[6].wait()
+    ints = my_integrals(integ, q * QUART)
+    for c in f_copies:
+        c.wait_recv()
+    most = fl[0]
+    for k in range(1, 8):
+        most = jnp.maximum(most, fl[k])
+    fl[8] = most
+    g_copies = [
+        remote(fl.at[8], fl.at[8 + k], g_send.at[k - 1], g_recv.at[k - 1], (x * 4 + (z + k) % 4, b))
+        for k in range(1, 4)
+    ]
+    for t in range(BLK):
+        build_coupled(vall, ints, coup, t * 64, t * 64 + 64)
+        y_copies[t].wait_recv()
+        away = at.at[(q + 2) % 4, t]
+        s_copies[t].append(remote(away, away, s_send.at[t, 1], s_recv.at[t, 1], (a, sibling)))
+    for c in g_copies:
+        c.wait_recv()
+    fl[12] = jnp.maximum(jnp.maximum(fl[8], fl[9]), jnp.maximum(fl[10], fl[11]))
+    g_copies += [
+        remote(fl.at[12], fl.at[12 + k], g_send.at[2 + k], g_recv.at[2 + k], ((x + k) % 4 * 4 + z, b))
+        for k in range(1, 4)
+    ]
+    for t in range(BLK):
+        for c in s_copies[t]:
+            c.wait_recv()
+        gather_rows(at, t1, gs, t)
+    pick(coup, gs, ps)
+    r_copies = []
+    for t in range(BLK):
+        part = add_rows(t2, ps, t).T
+        for k in range(8):
+            slab = part[k * SLAB : (k + 1) * SLAB]
+            sb[t, k] = slab
+            rb[t, 8 + k] = slab.astype(bf16)
+        r_copies.append([
+            remote(rb.at[t, 8 + m], rb.at[t, b], r_send.at[t, k], r_recv.at[t, k], (a, m))
+            for k, m in enumerate(peers)
+        ])
+    for t in range(BLK):
+        total = sb[t, b]
+        for k in range(1, 8):
+            r_copies[t][k - 1].wait_recv()
+            total = total + rb[t, (b + 8 - k) % 8].astype(f32)
+        out[:, t * ABLK : (t + 1) * ABLK] = total
+    for c in g_copies[3:]:
+        c.wait_recv()
+    flag_out[0] = jnp.max(fl[12:16])
+    for c in a_copies + v_copies + f_copies + g_copies + y_copies + sum(s_copies + r_copies, []):
+        c.wait_send()
 
 
 def assemble(local_amp, pair_src, num_local):
@@ -38,7 +360,7 @@
     return (combined, jnp.where(owner_dev == my_index, within, remote))
 
 
-def body(
+def by_links(
     amplitudes, integrals, beta_pair, beta_coef, pair_src, link_row, link_col, link_coef, link_count
 ):
     num_local = link_row.shape[0]
@@ -91,17 +413,63 @@
     return sigma_acc.reshape(num_local * ABLK, slab_piece)
 
 
+def body(amplitudes, integrals, beta_pair, beta_coef, pair_src, link_row, link_col, link_coef, link_count):
+    anym = pl.BlockSpec(memory_space=pl.ANY)
+    smem = pl.BlockSpec(memory_space=pltpu.SMEM)
+    vmem = pl.BlockSpec(memory_space=pltpu.VMEM)
+    rows = pltpu.VMEM((BLK * PAIRS, LINKS), f32)
+    dma = pltpu.SemaphoreType.DMA
+    sigma, most = pl.pallas_call(
+        kernel,
+        out_shape=(
+            jax.ShapeDtypeStruct((SLAB, BLK * ABLK), f32),
+            jax.ShapeDtypeStruct((1,), f32),
+        ),
+        in_specs=[anym] * 9,
+        out_specs=(vmem, smem),
+        scratch_shapes=[
+            pltpu.SMEM((PAIRS, ALPHA * BLK), i32),
+            pltpu.SMEM((BLK, PAIRS), i32),
+            pltpu.VMEM((SLAB, BLK * ABLK), bf16),
+            pltpu.VMEM((BLK, SLAB, ABLK), bf16),
+            pltpu.VMEM((ALPHA, FETCH_CAP, SLAB, ABLK), bf16),
+            pltpu.VMEM((NP, NP), f32),
+            pltpu.VMEM((SLAB, NB), i32),
+            pltpu.VMEM((SLAB, NB), f32),
+            pltpu.VMEM((BLK, PAIRS, LINKS), i32),
+            pltpu.VMEM((BLK, PAIRS, LINKS), i32),
+            pltpu.VMEM((BLK, PAIRS, LINKS), f32),
+            pltpu.VMEM((ALPHA * FETCH_CAP, SLAB, ABLK), bf16),
+            pltpu.VMEM((2, SLAB, HALF), f32),
+            pltpu.VMEM((NB, HALF), f32),
+            pltpu.VMEM((4, BLK, SLAB, PAIRS * ABLK), bf16),
+            pltpu.VMEM((NB * KROWS, HALF), f32),
+            rows, rows, rows, rows, rows, rows,
+            pltpu.VMEM((BLK, 128, 128), f32),
+            pltpu.VMEM((BLK, 32, 128), f32),
+            pltpu.VMEM((GROUPS * 4, BLK * CAP, HALF), bf16),
+            pltpu.VMEM((BLK, GROUPS * 4 * CAP, NB), bf16),
+            pltpu.VMEM((BLK, 8, SLAB, ABLK), f32),
+            pltpu.VMEM((BLK, 16, SLAB, ABLK), bf16),
+            pltpu.VMEM((16, 8, 128), f32),
+            dma((9,)), dma((15,)), dma((15,)), dma((7,)), dma((7,)), dma((BLK,)), dma((BLK,)),
+            dma((BLK, 2)), dma((BLK, 2)), dma((BLK, 7)), dma((BLK, 7)), dma((7,)), dma((7,)), dma((6,)), dma((6,)),
+        ],
+        compiler_params=pltpu.CompilerParams(
+            vmem_limit_bytes=60 << 20, collective_id=0, has_side_effects=True
+        ),
+        name="sigma_links",
+    )(amplitudes.T, integrals, beta_pair, beta_coef, pair_src.T, link_col, link_row, link_coef, link_count)
+    out = lax.cond(
+        most[0] >= CAP,
+        lambda: by_links(amplitudes, integrals, beta_pair, beta_coef, pair_src, link_row, link_col, link_coef,
+                         link_count).T,
+        lambda: sigma,
+    )
+    return out.T
+
+
 def solution(mesh):
-    in_specs = (
-        P("alpha", "beta"),
-        P(),
-        P("beta", None),
-        P("beta", None),
-        P(),
-        P("alpha", None, None),
-        P("alpha", None, None),
-        P("alpha", None, None),
-        P("alpha", None),
-    )
-    out_specs = P("alpha", "beta")
-    return jax.shard_map(body, mesh=mesh, in_specs=in_specs, out_specs=out_specs, check_vma=False)
+    in_specs = (P("alpha", "beta"), P(), P("beta", None), P("beta", None), P(),
+                P("alpha", None, None), P("alpha", None, None), P("alpha", None, None), P("alpha", None))
+    return jax.shard_map(body, mesh=mesh, in_specs=in_specs, out_specs=P("alpha", "beta"), check_vma=False)

time: 673 us -> 39.4 us (0.06)
  local copies, waits for them, and re-layouts: 355 us -> 0.86 us
  matrix products: 192 us -> 0 us
  loops' own time: 55.7 us -> 0.24 us
  Pallas kernels: 0 us -> 37.6 us
  other arithmetic: 29.7 us -> 0 us
  blocking collectives: 14.7 us -> 0 us
  waiting for transfers between devices: 14.1 us -> 0 us
  starting transfers between devices: 7.6 us -> 0 us
    gather x34 -> x0, local copies, waits for them, and re-layouts: 303 us -> none  [the longest x16 239 us: per_pair(): coupled_rows = jnp.take(coupled, orbital_pair, axis=0)]
    dot_general x34 -> x0, matrix products: 192 us -> none  [the longest x16 167 us: per_pair(): jnp.einsum('lbj,lj->lb', coupled_rows, amp_rows, preferred_element_type=j...]
    another operation x5 -> x1, loops' own time: 55.7 us -> 0.24 us  [body(): lax.cond(most[0] >= CAP, lambda: by_links(amplitudes, integrals, beta_pai...]
    pallas_call x0 -> x1, Pallas kernels: none -> 37.6 us  [body(): pl.pallas_call(kernel, out_shape=(jax.ShapeDtypeStruct((SLAB, BLK * ABLK)...]
    dynamic_slice x80 -> x0, local copies, waits for them, and re-layouts: 28.2 us -> none  [the longest x16 9.31 us: per_pair(): occupied[pair_index]]
    select_n x81 -> x0, other arithmetic: 27.2 us -> none  [the longest x16 13.6 us: per_pair(): block = jnp.take(gathered, chosen[pair_index], axis=0)]
    all_gather x1 -> x0, blocking collectives: 14.7 us -> none  [body(): full_rows = lax.all_gather(local_amp, 'beta', axis=2, tiled=True)]
    all_to_all x1 -> x0, waiting for transfers between devices: 14.1 us -> none  [assemble(): lax.all_to_all(outgoing, 'alpha', split_axis=0, concat_axis=0, tiled=True)]
  transfers between devices with their start and end apart: 1 -> 0, of which waited for: 1 -> 0; matrix products, arithmetic and copies ran while one was open for 2% -> 0% of each run, Pallas kernels for 0% -> 0%
where the time goes in v3:
time: 39.4 us; the launch traced here: 39.3 us
  Pallas kernels  37.6 us (95%)
  local copies, waits for them, and re-layouts  0.86 us (2%)
  between operations  0.63 us (2%)
    pallas_call x1, Pallas kernels, body(): pl.pallas_call(kernel, out_shape=(jax.ShapeDtypeStruct((SLAB, BLK * ABLK)...  37.6 us

profile of v3, /device:TPU:1, one launch (start us, length us, event | category | flops | bytes accessed | tf_op | source)
XLA Modules:
  0.0 39.3 jit_solution(16256174480589665455)
XLA Ops:
  0.0 37.6 %sigma_links.1 = (f32[32,512]{1,0:T(8,128)S(1)}, f32[1]{0:T(128)}) custom-call(bf16[32,512]{1,0:T(8,128)(2,1)} %bitcast.103, f32[324,324]{1,0:T(8,128)} %integ_h.1, s32[32,256]{1,0:T(8,128)} %pair_h.1, f32[32,256]{1,0:T(8,128)} %coef_h.1, s32[4,64]{1,0:T(4,128)} %bitcast.104, s32[4,4,1024]{2,1,0:T(4,128)} %col_h.1, s32[4,4,1024]{2,1,0:T(4,128)} %row_h.1, ...), custom_call_target="tpu_custom_call" | custom-call | tf_op jit(solution)/shard_map/sigma_links/pallas_call | solution.py:422
  38.2 0.4 conditional.1
  38.2 0.1 copy.38
  38.5 0.7 %copy.40 = f32[32,512]{1,0:T(8,128)} copy(f32[32,512]{0,1:T(8,128)S(1)} %get-tuple-element.964) | data formatting | bytes 131072 | tf_op jit(solution)/shard_map/cond | solution.py:463

commit v4 on v3

--- a/solution.py
+++ b/solution.py
@@ -21,6 +21,8 @@
 CAP = 32
 GROUPS = 21
 GCHUNK = 7
+CHUNKS = 2
+SPAN = BLK // CHUNKS
 NTDIMS = (((1,), (1,)), ((), ()))
 f32, bf16, i32 = jnp.float32, jnp.bfloat16, jnp.int32
 MESH = pl.DeviceIdType.MESH
@@ -112,7 +114,7 @@
         return tuple(carry)
 
     zero = jnp.zeros((KROWS, 128), f32)
-    lax.fori_loop(0, PAIRS, one, (zero,) * BLK)
+    lax.fori_loop(0, PAIRS, one, (zero,) * BLK, unroll=2)
 
 
 def fill_tables(lo, hi, u1, u2, t1, t2):
@@ -134,7 +136,7 @@
         t2[t] = a2
         return carry
 
-    lax.fori_loop(0, BLK, target, 0)
+    lax.fori_loop(0, BLK, target, 0, unroll=2)
 
 
 def gather_rows(at, t1, gs, t):
@@ -187,6 +189,7 @@
     sibling = b // 2 * 2 + 1 - core
     across = half * 4 + (q + 2) % 4
     peers = [(b + k) % 8 for k in range(1, 8)]
+    mates = [half * 4 + (q + k) % 4 for k in range(1, 4)]
 
     loads = []
     for n, (h, m) in enumerate([(amp_h, amp), (pair_h, pair), (coef_h, coef), (col_h, col), (row_h, row),
@@ -255,9 +258,9 @@
     ok = (kl >= 0) & (r < CAP)
     lo[...] = jnp.where(ok, (kl & 3) * CAP + r, -1).astype(f32)
     hi[...] = jnp.where(ok, kl >> 2, -1).astype(f32)
-    fl[b] = jnp.broadcast_to(jnp.max(rank[...], keepdims=True), (8, 128))
+    fl[q] = jnp.broadcast_to(jnp.max(rank[...], keepdims=True), (8, 128))
     f_copies = [
-        remote(fl.at[b], fl.at[b], f_send.at[k], f_recv.at[k], (a, m)) for k, m in enumerate(peers)
+        remote(fl.at[q], fl.at[q], f_send.at[k], f_recv.at[k], (a, m)) for k, m in enumerate(mates)
     ]
     fill_tables(lo, hi, u1, u2, t1, t2)
 
@@ -272,9 +275,11 @@
             at[q, t, :, p * ABLK : (p + 1) * ABLK] = ev[
                 owner * FETCH_CAP + jnp.where(below != 0, 1, 0)
             ]
-        mine = at.at[q, t]
-        y_copies.append(remote(mine, mine, y_send.at[t], y_recv.at[t], (a, across)))
-        s_copies.append([remote(mine, mine, s_send.at[t, 0], s_recv.at[t, 0], (a, sibling))])
+        if t % 2:
+            pair = pl.ds(t - 1, 2)
+            mine, n = at.at[q, pair], t // 2
+            y_copies.append(remote(mine, mine, y_send.at[n], y_recv.at[n], (a, across)))
+            s_copies.append([remote(mine, mine, s_send.at[n, 0], s_recv.at[n, 0], (a, sibling))])
 
     for c in v_copies:
         c.wait_recv()
@@ -282,19 +287,19 @@
     ints = my_integrals(integ, q * QUART)
     for c in f_copies:
         c.wait_recv()
-    most = fl[0]
-    for k in range(1, 8):
-        most = jnp.maximum(most, fl[k])
-    fl[8] = most
+    fl[8] = jnp.maximum(jnp.maximum(fl[0], fl[1]), jnp.maximum(fl[2], fl[3]))
     g_copies = [
         remote(fl.at[8], fl.at[8 + k], g_send.at[k - 1], g_recv.at[k - 1], (x * 4 + (z + k) % 4, b))
         for k in range(1, 4)
     ]
     for t in range(BLK):
         build_coupled(vall, ints, coup, t * 64, t * 64 + 64)
-        y_copies[t].wait_recv()
-        away = at.at[(q + 2) % 4, t]
-        s_copies[t].append(remote(away, away, s_send.at[t, 1], s_recv.at[t, 1], (a, sibling)))
+        if t in (1, 2):
+            y_copies[t - 1].wait_recv()
+            away = at.at[(q + 2) % 4, pl.ds(t * 2 - 2, 2)]
+            s_copies[t - 1].append(
+                remote(away, away, s_send.at[t - 1, 1], s_recv.at[t - 1, 1], (a, sibling))
+            )
     for c in g_copies:
         c.wait_recv()
     fl[12] = jnp.maximum(jnp.maximum(fl[8], fl[9]), jnp.maximum(fl[10], fl[11]))
@@ -303,31 +308,35 @@
         for k in range(1, 4)
     ]
     for t in range(BLK):
-        for c in s_copies[t]:
-            c.wait_recv()
+        if t % 2 == 0:
+            for c in s_copies[t // 2]:
+                c.wait_recv()
         gather_rows(at, t1, gs, t)
     pick(coup, gs, ps)
     r_copies = []
-    for t in range(BLK):
-        part = add_rows(t2, ps, t).T
+    for n in range(CHUNKS):
+        parts = [add_rows(t2, ps, n * SPAN + i).T for i in range(SPAN)]
         for k in range(8):
-            slab = part[k * SLAB : (k + 1) * SLAB]
-            sb[t, k] = slab
-            rb[t, 8 + k] = slab.astype(bf16)
+            slab = jnp.concatenate([part[k * SLAB : (k + 1) * SLAB] for part in parts], axis=1)
+            sb[n, k] = slab
+            rb[n, 8 + k] = slab.astype(bf16)
         r_copies.append([
-            remote(rb.at[t, 8 + m], rb.at[t, b], r_send.at[t, k], r_recv.at[t, k], (a, m))
-            for k, m in enumerate(peers)
+            remote(rb.at[n, 8 + peers[k]], rb.at[n, b], r_send.at[n, k], r_recv.at[n, k], (a, peers[k]))
+            for k in (3, 2, 4, 1, 5, 0, 6)
         ])
-    for t in range(BLK):
-        total = sb[t, b]
+    for c in a_copies + v_copies + f_copies + g_copies + y_copies + sum(s_copies, []):
+        c.wait_send()
+    for n in range(CHUNKS):
+        for c in r_copies[n]:
+            c.wait_recv()
+        total = sb[n, b]
         for k in range(1, 8):
-            r_copies[t][k - 1].wait_recv()
-            total = total + rb[t, (b + 8 - k) % 8].astype(f32)
-        out[:, t * ABLK : (t + 1) * ABLK] = total
+            total = total + rb[n, (b + 8 - k) % 8].astype(f32)
+        out[:, n * SPAN * ABLK : (n + 1) * SPAN * ABLK] = total
     for c in g_copies[3:]:
         c.wait_recv()
     flag_out[0] = jnp.max(fl[12:16])
-    for c in a_copies + v_copies + f_copies + g_copies + y_copies + sum(s_copies + r_copies, []):
+    for c in sum(r_copies, []):
         c.wait_send()
 
 
@@ -449,11 +458,11 @@
             pltpu.VMEM((BLK, 32, 128), f32),
             pltpu.VMEM((GROUPS * 4, BLK * CAP, HALF), bf16),
             pltpu.VMEM((BLK, GROUPS * 4 * CAP, NB), bf16),
-            pltpu.VMEM((BLK, 8, SLAB, ABLK), f32),
-            pltpu.VMEM((BLK, 16, SLAB, ABLK), bf16),
+            pltpu.VMEM((CHUNKS, 8, SLAB, SPAN * ABLK), f32),
+            pltpu.VMEM((CHUNKS, 16, SLAB, SPAN * ABLK), bf16),
             pltpu.VMEM((16, 8, 128), f32),
-            dma((9,)), dma((15,)), dma((15,)), dma((7,)), dma((7,)), dma((BLK,)), dma((BLK,)),
-            dma((BLK, 2)), dma((BLK, 2)), dma((BLK, 7)), dma((BLK, 7)), dma((7,)), dma((7,)), dma((6,)), dma((6,)),
+            dma((9,)), dma((15,)), dma((15,)), dma((7,)), dma((7,)), dma((2,)), dma((2,)),
+            dma((2, 2)), dma((2, 2)), dma((CHUNKS, 7)), dma((CHUNKS, 7)), dma((3,)), dma((3,)), dma((6,)), dma((6,)),
         ],
         compiler_params=pltpu.CompilerParams(
             vmem_limit_bytes=60 << 20, collective_id=0, has_side_effects=True

time: 39.4 us -> 35.6 us (0.904)
  Pallas kernels: 37.6 us -> 33.7 us
    pallas_call x1, Pallas kernels: 37.6 us -> 33.7 us  [body(): pl.pallas_call(kernel, out_shape=(jax.ShapeDtypeStruct((SLAB, BLK * ABLK)...]
where the time goes in v4:
time: 35.6 us; the launch traced here: 35.4 us
  Pallas kernels  33.7 us (95%)
  local copies, waits for them, and re-layouts  0.86 us (2%)
  between operations  0.63 us (2%)
    pallas_call x1, Pallas kernels, body(): pl.pallas_call(kernel, out_shape=(jax.ShapeDtypeStruct((SLAB, BLK * ABLK)...  33.7 us
    cond x1, local copies, waits for them, and re-layouts, body(): lax.cond(most[0] >= CAP, lambda: by_links(amplitudes, integrals, beta_pai...  0.74 us

profile of v4, /device:TPU:1, one launch (start us, length us, event | category | flops | bytes accessed | tf_op | source)
XLA Modules:
  0.0 35.4 jit_solution(557147274321009394)
XLA Ops:
  0.0 33.7 %sigma_links.1 = (f32[32,512]{1,0:T(8,128)S(1)}, f32[1]{0:T(128)}) custom-call(bf16[32,512]{1,0:T(8,128)(2,1)} %bitcast.103, f32[324,324]{1,0:T(8,128)} %integ_h.1, s32[32,256]{1,0:T(8,128)} %pair_h.1, f32[32,256]{1,0:T(8,128)} %coef_h.1, s32[4,64]{1,0:T(4,128)} %bitcast.104, s32[4,4,1024]{2,1,0:T(4,128)} %col_h.1, s32[4,4,1024]{2,1,0:T(4,128)} %row_h.1, ...), custom_call_target="tpu_custom_call" | custom-call | tf_op jit(solution)/shard_map/sigma_links/pallas_call | solution.py:431
  34.3 0.4 %conditional.1 = (f32[32,512]{0,1:T(8,128)S(1)}) conditional(s32[]{:T(128)} %bitcast.10, f32[32,512]{1,0:T(8,128)S(1)} %get-tuple-element.482, (s32[64,4]{0,1:T(4,128)}, bf16[512,32]{0,1:T(8,128)(2,1)}, s32[32,256]{1,0:T(8,128)}, f32[324,324]{1,0:T(8,128)}, f32[32,256]{1,0:T(8,128)}, /*index=5*/s32[4,4,1024]{2,1,0:T(4,128)}, s32[4,4]{1,0:T(4,128)}, ...), branch_computations={%region_0.0_spmd, %region_1.10_spmd} | conditional | flops 10414175232 | bytes 91081208 | solution.py:472
  34.3 0.1 copy.38
  34.7 0.7 %copy.40 = f32[32,512]{1,0:T(8,128)} copy(f32[32,512]{0,1:T(8,128)S(1)} %get-tuple-element.964) | data formatting | bytes 131072 | tf_op jit(solution)/shard_map/cond | solution.py:472

commit v5 on v4

--- a/solution.py
+++ b/solution.py
@@ -44,23 +44,15 @@
     return mask.astype(f32).astype(bf16)
 
 
-def wanted(src, device, owner):
-    bits = jnp.int32(0)
+def asked_range(src, device, first):
+    low, high = jnp.int32(BLK - 1), jnp.int32(0)
     for t in range(BLK):
         for p in range(PAIRS):
-            block = src[p, device * BLK + t]
-            bits = bits | jnp.where((block >> 2) == owner, bit_of(block & 3), 0)
-    return bits
-
-
-def bit_of(j):
-    return jnp.where(j == 0, 1, jnp.where(j == 1, 2, jnp.where(j == 2, 4, 8)))
-
-
-def lowest(bits):
-    return jnp.where(
-        (bits & 1) != 0, 0, jnp.where((bits & 2) != 0, 1, jnp.where((bits & 4) != 0, 2, 3))
-    )
+            j = src[p, device * BLK + t] - first
+            here = (j >> 2) == 0
+            low = jnp.minimum(low, jnp.where(here, j, BLK - 1))
+            high = jnp.maximum(high, jnp.where(here, j, 0))
+    return low, high
 
 
 def my_integrals(integ, first):
@@ -88,7 +80,7 @@
             coup[pl.ds(start, KROWS), :] = out[:, h * HALF : (h + 1) * HALF]
         return carry
 
-    lax.fori_loop(begin // 2, end // 2, one, 0, unroll=16)
+    lax.fori_loop(begin // 2, end // 2, one, 0, unroll=32)
 
 
 def rank_links(klq, rank):
@@ -140,22 +132,26 @@
 
 
 def gather_rows(at, t1, gs, t):
-    tables = [((128 + iota((128, 128), 1)) * (1 << p)).astype(f32) for p in range(PAIRS)]
+    tables = [((128 + iota((128, 128), 1)) * (1 << p)).astype(f32) for p in range(2)]
     amps = at[:, t].reshape(HALF, PAIRS * ABLK)
+    amps = jnp.concatenate([amps[:, : 2 * ABLK], amps[:, 2 * ABLK :]], axis=0)
     for c in range(GROUPS // GCHUNK):
-        hots = []
+        hots, later = [], []
         for h in range(GCHUNK):
             code = jnp.take_along_axis(t1[t], jnp.full((128, 128), c * GCHUNK + h, i32), axis=1)
             size = jnp.abs(code)
             sign = jnp.where(code < 0.0, -1.0, 1.0)
+            later.append(size >= 512.0)
+            size = jnp.where(later[h], size * 0.25, size)
             hots.append(
                 jnp.concatenate([jnp.where(size == tab, sign, 0.0).astype(bf16) for tab in tables], axis=1)
             )
-        rows = dot_nt(jnp.concatenate(hots, axis=0), amps).astype(bf16)
+        both = dot_nt(jnp.concatenate(hots, axis=0), amps)
         for h in range(GCHUNK):
+            two = both[h * 128 : (h + 1) * 128]
+            rows = jnp.where(later[h], two[:, HALF:], two[:, :HALF]).astype(bf16)
             for k in range(4):
-                s = h * 128 + k * CAP
-                gs[(c * GCHUNK + h) * 4 + k, t * CAP : (t + 1) * CAP, :] = rows[s : s + CAP]
+                gs[(c * GCHUNK + h) * 4 + k, t * CAP : (t + 1) * CAP, :] = rows[k * CAP : (k + 1) * CAP]
 
 
 def pick(coup, gs, ps):
@@ -191,6 +187,11 @@
     peers = [(b + k) % 8 for k in range(1, 8)]
     mates = [half * 4 + (q + k) % 4 for k in range(1, 4)]
 
+    offsets = sorted(
+        ((dx, dz) for dx in range(4) for dz in range(4)),
+        key=lambda d: (-min(d[0], 4 - d[0]) - min(d[1], 4 - d[1]), d),
+    )
+
     loads = []
     for n, (h, m) in enumerate([(amp_h, amp), (pair_h, pair), (coef_h, coef), (col_h, col), (row_h, row),
                                 (lcoef_h, lcoef), (integ_h, integ), (src_h, src),
@@ -208,24 +209,11 @@
     loads[7].wait()
     for j in range(BLK):
         blocks[j] = amp[:, j * ABLK : (j + 1) * ABLK]
-    for k in range(ALPHA):
-        asked = wanted(src, (a + k) % ALPHA, a)
-        low = lowest(asked)
-        for n, j in enumerate((low, lowest(asked - bit_of(low)))):
+    for k, (dx, dz) in enumerate(offsets):
+        to = (x + dx) % 4 * 4 + (z + dz) % 4
+        for n, j in enumerate(asked_range(src, to, a * BLK)):
             give[k, n] = blocks[j]
-    ev[pl.ds(a * FETCH_CAP, FETCH_CAP)] = give[0]
-    pl.semaphore_wait(barrier, ALPHA - 1 + 7)
-
-    def remote(source, target, send, recv, to):
-        c = pltpu.make_async_remote_copy(src_ref=source, dst_ref=target, send_sem=send, recv_sem=recv,
-                                         device_id=to, device_id_type=MESH)
-        c.start()
-        return c
-
-    a_copies = [
-        remote(give.at[k], ev.at[pl.ds(a * FETCH_CAP, FETCH_CAP)], a_send.at[k - 1], a_recv.at[k - 1], ((a + k) % ALPHA, b))
-        for k in range(1, ALPHA)
-    ]
+    ev[pl.ds(a * FETCH_CAP, FETCH_CAP)] = give[ALPHA - 1]
     loads[1].wait()
     loads[2].wait()
     mine = pl.ds(pl.multiple_of(b * SLAB, SLAB), SLAB)
@@ -233,9 +221,31 @@
     for h in range(2):
         vown[h] = codes[:, h * HALF : (h + 1) * HALF]
     vall[mine, :] = vown[half]
+    pl.semaphore_wait(barrier, ALPHA - 1 + 7)
+
+    def remote(source, target, send, recv, to):
+        c = pltpu.make_async_remote_copy(src_ref=source, dst_ref=target, send_sem=send, recv_sem=recv,
+                                         device_id=to, device_id_type=MESH)
+        c.start()
+        return c
+
+    a_copies = [
+        remote(give.at[k], ev.at[pl.ds(a * FETCH_CAP, FETCH_CAP)], a_send.at[k], a_recv.at[k],
+               ((x + dx) % 4 * 4 + (z + dz) % 4, b))
+        for k, (dx, dz) in enumerate(offsets[:-1])
+    ]
     v_copies = [
         remote(vown.at[m // 4], vall.at[mine], v_send.at[k], v_recv.at[k], (a, m)) for k, m in enumerate(peers)
     ]
+
+    asked = [src[p, a * BLK + t] for t in range(BLK) for p in range(PAIRS)]
+    owners = [block >> 2 for block in asked]
+    places = []
+    for block, owner in zip(asked, owners):
+        low = block
+        for other, its in zip(asked, owners):
+            low = jnp.minimum(low, jnp.where(its == owner, other, block))
+        places.append(owner * FETCH_CAP + jnp.where(low == block, 0, 1))
 
     for n in (3, 4, 5, 8):
         loads[n].wait()
@@ -264,17 +274,14 @@
     ]
     fill_tables(lo, hi, u1, u2, t1, t2)
 
+    loads[6].wait()
+    ints = my_integrals(integ, q * QUART)
     for c in a_copies:
         c.wait_recv()
     y_copies, s_copies = [], []
     for t in range(BLK):
         for p in range(PAIRS):
-            block = src[p, a * BLK + t]
-            owner = block >> 2
-            below = wanted(src, a, owner) & (bit_of(block & 3) - 1)
-            at[q, t, :, p * ABLK : (p + 1) * ABLK] = ev[
-                owner * FETCH_CAP + jnp.where(below != 0, 1, 0)
-            ]
+            at[q, t, :, p * ABLK : (p + 1) * ABLK] = ev[places[t * PAIRS + p]]
         if t % 2:
             pair = pl.ds(t - 1, 2)
             mine, n = at.at[q, pair], t // 2
@@ -283,8 +290,6 @@
 
     for c in v_copies:
         c.wait_recv()
-    loads[6].wait()
-    ints = my_integrals(integ, q * QUART)
     for c in f_copies:
         c.wait_recv()
     fl[8] = jnp.maximum(jnp.maximum(fl[0], fl[1]), jnp.maximum(fl[2], fl[3]))

time: 35.6 us -> 34.1 us (0.958)
  Pallas kernels: 33.7 us -> 32.3 us
    pallas_call x1, Pallas kernels: 33.7 us -> 32.3 us  [body(): pl.pallas_call(kernel, out_shape=(jax.ShapeDtypeStruct((SLAB, BLK * ABLK)...]
where the time goes in v5:
time: 34.1 us; the launch traced here: 34 us
  Pallas kernels  32.3 us (95%)
  local copies, waits for them, and re-layouts  0.86 us (3%)
  between operations  0.63 us (2%)
    pallas_call x1, Pallas kernels, body(): pl.pallas_call(kernel, out_shape=(jax.ShapeDtypeStruct((SLAB, BLK * ABLK)...  32.3 us
    cond x1, local copies, waits for them, and re-layouts, body(): lax.cond(most[0] >= CAP, lambda: by_links(amplitudes, integrals, beta_pai...  0.74 us

profile of v5, /device:TPU:1, one launch (start us, length us, event | category | flops | bytes accessed | tf_op | source)
XLA Modules:
  0.0 34.0 jit_solution(787784507442279063)
XLA Ops:
  0.0 32.3 %sigma_links.1 = (f32[32,512]{1,0:T(8,128)S(1)}, f32[1]{0:T(128)}) custom-call(bf16[32,512]{1,0:T(8,128)(2,1)} %bitcast.103, f32[324,324]{1,0:T(8,128)} %integ_h.1, s32[32,256]{1,0:T(8,128)} %pair_h.1, f32[32,256]{1,0:T(8,128)} %coef_h.1, s32[4,64]{1,0:T(4,128)} %bitcast.104, s32[4,4,1024]{2,1,0:T(4,128)} %col_h.1, s32[4,4,1024]{2,1,0:T(4,128)} %row_h.1, ...), custom_call_target="tpu_custom_call" | custom-call | tf_op jit(solution)/shard_map/sigma_links/pallas_call | solution.py:436
  32.9 0.4 %conditional.1 = (f32[32,512]{0,1:T(8,128)S(1)}) conditional(s32[]{:T(128)} %bitcast.10, f32[32,512]{1,0:T(8,128)S(1)} %get-tuple-element.482, (s32[64,4]{0,1:T(4,128)}, bf16[512,32]{0,1:T(8,128)(2,1)}, s32[32,256]{1,0:T(8,128)}, f32[324,324]{1,0:T(8,128)}, f32[32,256]{1,0:T(8,128)}, /*index=5*/s32[4,4,1024]{2,1,0:T(4,128)}, s32[4,4]{1,0:T(4,128)}, ...), branch_computations={%region_0.0_spmd, %region_1.10_spmd} | conditional | flops 10414175232 | bytes 91081208 | solution.py:477
  32.9 0.1 copy.38
  33.2 0.7 %copy.40 = f32[32,512]{1,0:T(8,128)} copy(f32[32,512]{0,1:T(8,128)S(1)} %get-tuple-element.964) | data formatting | bytes 131072 | tf_op jit(solution)/shard_map/cond | solution.py:477

commit v6 on v5

--- a/solution.py
+++ b/solution.py
@@ -106,7 +106,7 @@
         return tuple(carry)
 
     zero = jnp.zeros((KROWS, 128), f32)
-    lax.fori_loop(0, PAIRS, one, (zero,) * BLK, unroll=2)
+    lax.fori_loop(0, PAIRS, one, (zero,) * BLK, unroll=4)
 
 
 def fill_tables(lo, hi, u1, u2, t1, t2):
@@ -128,7 +128,7 @@
         t2[t] = a2
         return carry
 
-    lax.fori_loop(0, BLK, target, 0, unroll=2)
+    lax.fori_loop(0, BLK, target, 0, unroll=4)
 
 
 def gather_rows(at, t1, gs, t):
@@ -299,11 +299,11 @@
     ]
     for t in range(BLK):
         build_coupled(vall, ints, coup, t * 64, t * 64 + 64)
-        if t in (1, 2):
-            y_copies[t - 1].wait_recv()
-            away = at.at[(q + 2) % 4, pl.ds(t * 2 - 2, 2)]
-            s_copies[t - 1].append(
-                remote(away, away, s_send.at[t - 1, 1], s_recv.at[t - 1, 1], (a, sibling))
+        if t in (2, 3):
+            y_copies[t - 2].wait_recv()
+            away = at.at[(q + 2) % 4, pl.ds(t * 2 - 4, 2)]
+            s_copies[t - 2].append(
+                remote(away, away, s_send.at[t - 2, 1], s_recv.at[t - 2, 1], (a, sibling))
             )
     for c in g_copies:
         c.wait_recv()
@@ -457,7 +457,7 @@
             pltpu.VMEM((2, SLAB, HALF), f32),
             pltpu.VMEM((NB, HALF), f32),
             pltpu.VMEM((4, BLK, SLAB, PAIRS * ABLK), bf16),
-            pltpu.VMEM((NB * KROWS, HALF), f32),
+            pltpu.VMEM((NB * KROWS + KROWS, HALF), f32),
             rows, rows, rows, rows, rows, rows,
             pltpu.VMEM((BLK, 128, 128), f32),
             pltpu.VMEM((BLK, 32, 128), f32),

time: 34.1 us -> 33.6 us (0.985)
  Pallas kernels: 32.3 us -> 31.9 us
where the time goes in v6:
time: 33.6 us; the launch traced here: 33.4 us
  Pallas kernels  31.9 us (95%)
  local copies, waits for them, and re-layouts  0.86 us (3%)
  between operations  0.63 us (2%)
    pallas_call x1, Pallas kernels, body(): pl.pallas_call(kernel, out_shape=(jax.ShapeDtypeStruct((SLAB, BLK * ABLK)...  31.9 us
    cond x1, local copies, waits for them, and re-layouts, body(): lax.cond(most[0] >= CAP, lambda: by_links(amplitudes, integrals, beta_pai...  0.74 us

profile of v6, /device:TPU:1, one launch (start us, length us, event | category | flops | bytes accessed | tf_op | source)
XLA Modules:
  0.0 33.4 jit_solution(4935688149521580170)
XLA Ops:
  0.0 31.9 %sigma_links.1 = (f32[32,512]{1,0:T(8,128)S(1)}, f32[1]{0:T(128)}) custom-call(bf16[32,512]{1,0:T(8,128)(2,1)} %bitcast.103, f32[324,324]{1,0:T(8,128)} %integ_h.1, s32[32,256]{1,0:T(8,128)} %pair_h.1, f32[32,256]{1,0:T(8,128)} %coef_h.1, s32[4,64]{1,0:T(4,128)} %bitcast.104, s32[4,4,1024]{2,1,0:T(4,128)} %col_h.1, s32[4,4,1024]{2,1,0:T(4,128)} %row_h.1, ...), custom_call_target="tpu_custom_call" | custom-call | tf_op jit(solution)/shard_map/sigma_links/pallas_call | solution.py:436
  32.6 0.1 conditional.1
  32.6 0.1 copy.38
  32.7 0.7 %copy.40 = f32[32,512]{1,0:T(8,128)} copy(f32[32,512]{0,1:T(8,128)S(1)} %get-tuple-element.964) | data formatting | bytes 131072 | tf_op jit(solution)/shard_map/cond | solution.py:477
